TPU v7x, 32 devices: a whole 2x2x4 slice. The times are simulated.
32 devices in a mesh: wide: 8 (over z, y), narrow: 4 (over x, core).
Axes of the slice: x: 2, y: 2, z: 4, core: 2. Of those that a mesh axis runs over, the one named last changes fastest.
Arguments:
- loads: float32 [32, 8, 8, 512], P('wide', 'narrow'), may hold values from -6 to 6
- schur: float32 [32, 8, 512, 512], P('wide', 'narrow'), as said below
- local_inverse: float32 [32, 8, 512, 512], P('wide', 'narrow'), as said below
- coarse_basis: float32 [32, 8, 16, 512], P('wide', 'narrow'), may hold values from -0.6 to 0.6
- coarse_inverse: float32 [2176, 2176], P('wide', 'narrow'), may hold values from -0.125 to 0.125
- coarse_index: int32 [32, 8, 16], P('wide', 'narrow'), may hold values from 0 to 2175, as said below
Outputs:
- solution: float32 [32, 8, 8, 512], P('wide', 'narrow')
- residual: float32 [32, 8, 8, 512], P('wide', 'narrow')
Inputs may be any that keep to these rules, and one draw needn't show every extreme that they name: `coarse_index`: the 4 coarse dofs of a face (local positions f * 4 to f * 4 + 3 for face f in the order west, east, south, north) carry one global number each; a face shared by two subdomains has the same numbers on both sides, and every number of 0 to 2175 belongs to exactly one face. `schur`: each subdomain's block is symmetric with a dominant positive diagonal. `local_inverse`: each subdomain's block is symmetric with a dominant positive diagonal.
All inputs are finite; a program needn't handle non-finite values.
Results may differ from a plain program's by a relative error of at most 0.0001.
Values sent between devices are 32-bit elements; how exact they have to be, the bound alone decides.
A program may use at most 128 MiB of HBM per device.

v0:
```python
import jax
import jax.numpy as jnp
from jax import lax
from jax.sharding import PartitionSpec as P

ITERS = 2


def padded(block, sides, width, periodic):
    for axis, dim in sides:
        count = lax.axis_size(axis)
        forward = [(i, i + 1) for i in range(count - 1)]
        if periodic:
            forward.append((count - 1, 0))
        backward = [(target, source) for source, target in forward]
        low = lax.ppermute(
            lax.slice_in_dim(block, block.shape[dim] - width, None, axis=dim), axis, forward
        )
        high = lax.ppermute(lax.slice_in_dim(block, 0, width, axis=dim), axis, backward)
        block = jnp.concatenate([low, block, high], axis=dim)
    return block


def face_weights(position, total, face_width):
    south_weight = jnp.where(position == 0, 1.0, 0.5)
    north_weight = jnp.where(position == total - 1, 1.0, 0.5)
    halves = jnp.full((position.shape[0], face_width), 0.5, jnp.float32)
    ones_row = jnp.ones((position.shape[0], face_width), jnp.float32)
    return jnp.concatenate(
        [halves, halves, south_weight[:, None] * ones_row, north_weight[:, None] * ones_row], axis=1
    )


def face_sum(field):
    face_width = field.shape[3] // 4
    west_part = field[..., 0:face_width]
    east_part = field[..., face_width : 2 * face_width]
    south_part = field[..., 2 * face_width : 3 * face_width]
    north_part = field[..., 3 * face_width :]
    padded_hoop = padded(field, (("wide", 0),), 1, True)
    before_east = padded_hoop[:-2, ..., face_width : 2 * face_width]
    after_west = padded_hoop[2:, ..., 0:face_width]
    padded_across = padded(field, (("narrow", 1),), 1, False)
    below_north = padded_across[:, :-2, ..., 3 * face_width :]
    above_south = padded_across[:, 2:, ..., 2 * face_width : 3 * face_width]
    return jnp.concatenate(
        [
            west_part + before_east,
            east_part + after_west,
            south_part + below_north,
            north_part + above_south,
        ],
        axis=3,
    )


def apply_blocks(blocks, field):
    return jnp.einsum("abij,ablj->abli", blocks, field, precision=lax.Precision.HIGHEST)


def per_device(loads, schur, local_inverse, coarse_basis, coarse_inverse, coarse_index):
    sub_circ = loads.shape[0]
    sub_across = loads.shape[1]
    load_count = loads.shape[2]
    face_width = loads.shape[3] // 4
    coarse_count = coarse_basis.shape[2]
    column_block = coarse_inverse.shape[1]
    narrow_position = lax.axis_index("narrow")
    across_total = sub_across * lax.axis_size("narrow")
    across_position = narrow_position * sub_across + lax.iota(jnp.int32, sub_across)
    inv_mult = face_weights(across_position, across_total, face_width)[None, :, None, :]
    coarse_total = column_block * lax.axis_size("narrow")
    local_numbers = coarse_index.reshape(-1)
    all_numbers = lax.all_gather(local_numbers, ("wide", "narrow"), axis=0, tiled=True)
    solution = jnp.zeros_like(loads)
    for iteration in range(ITERS):
        if iteration == 0:
            current = face_sum(loads)
        else:
            current = face_sum(loads - apply_blocks(schur, solution))
        weighted = current * inv_mult
        restricted = jnp.einsum(
            "abli,abki->labk", weighted, coarse_basis, precision=lax.Precision.HIGHEST
        )
        restricted = restricted.reshape(load_count, -1)
        gathered = lax.all_gather(restricted, ("wide", "narrow"), axis=1, tiled=True)
        coarse_rhs = (
            jnp.zeros((load_count, coarse_total), jnp.float32).at[:, all_numbers].add(gathered)
        )
        rhs_columns = lax.dynamic_slice_in_dim(
            coarse_rhs, narrow_position * column_block, column_block, 1
        )
        partial_rows = jnp.einsum(
            "lc,rc->lr", rhs_columns, coarse_inverse, precision=lax.Precision.HIGHEST
        )
        row_block = lax.psum(partial_rows, "narrow")
        coarse_sol = lax.all_gather(row_block, "wide", axis=1, tiled=True)
        picked = jnp.take(coarse_sol, local_numbers, axis=1).reshape(
            load_count, sub_circ, sub_across, coarse_count
        )
        correction = apply_blocks(local_inverse, weighted) + jnp.einsum(
            "labk,abki->abli", picked, coarse_basis, precision=lax.Precision.HIGHEST
        )
        solution = solution + face_sum(correction) * inv_mult
    residual = face_sum(loads - apply_blocks(schur, solution))
    return (solution, residual)


def solution(mesh):
    return jax.shard_map(
        per_device,
        mesh=mesh,
        in_specs=(
            P("wide", "narrow", None, None),
            P("wide", "narrow", None, None),
            P("wide", "narrow", None, None),
            P("wide", "narrow", None, None),
            P("wide", "narrow"),
            P("wide", "narrow", None),
        ),
        out_specs=(P("wide", "narrow", None, None), P("wide", "narrow", None, None)),
        check_vma=False,
    )
```

profile of v0, /device:TPU:0, one launch (start us, length us, event | category | flops | bytes accessed | tf_op | source)
XLA Modules:
  0.0 358.7 jit_solution(17238945854583764441)
XLA Ops:
  1.5 3.0 collective-permute-start
  4.5 3.1 collective-permute-start.1
  8.4 1.5 collective-permute-start.2
  13.4 41.8 %all-gather = s32[32,1,128]{2,1,0:T(1,128)S(1)} all-gather(s32[1,1,128]{2,1,0:T(1,128)S(1)} %reshape.76), channel_id=1, replica_groups=mesh['wide'=8,'narrow'=4] {'wide','narrow'}, dimensions={0}, use_global_device_ids=true | all-gather | bytes 16896 | tf_op jit(solution)/shard_map/all_gather | solution.py:74
  56.9 1.3 convolution_bitcast_fusion.1
  58.4 36.9 %all_gather.16 = f32[8,4096]{1,0:T(8,128)S(1)} all-gather(f32[8,128]{1,0:T(8,128)S(1)} %reshape.36), channel_id=1, replica_groups=mesh['wide'=8,'narrow'=4] {'wide','narrow'}, dimensions={1}, use_global_device_ids=true | all-gather | bytes 135168 | tf_op jit(solution)/shard_map/all_gather | solution.py:86
  95.9 23.5 %scatter_custom_fusion = f32[8,2176]{0,1:T(8,128)} fusion(s32[4096]{0:T(1024)} %compare_select_fusion, f32[4096,8]{1,0:T(8,128)S(1)} %copy.21, f32[]{:T(128)} %constant.4.clone.1), kind=kCustom, calls=%fused_computation.12 | custom fusion | flops 32768 | bytes 70144 | tf_op jit(solution)/shard_map/scatter-add | solution.py:88
  119.4 2.0 fusion.6
  121.4 11.6 %psum.14 = f32[8,272]{1,0:T(8,128)S(1)} all-reduce(f32[8,272]{1,0:T(8,128)S(1)} %fusion.6), channel_id=1, replica_groups=mesh['wide'=8,'narrow'=4] {'narrow'}, use_global_device_ids=true, to_apply=%region_1.2 | all-reduce | flops 2176 | bytes 17408 | tf_op jit(solution)/shard_map/psum | solution.py:96
  133.0 30.5 %all-gather.1 = f32[8,272,8]{1,2,0:T(8,128)S(1)} all-gather(f32[1,272,8]{1,2,0:T(8,128)S(1)} %bitcast.45), channel_id=1, replica_groups=mesh['wide'=8,'narrow'=4] {'wide'}, dimensions={0}, use_global_device_ids=true | all-gather | bytes 78336 | tf_op jit(solution)/shard_map/all_gather | solution.py:97
  165.0 9.2 %convolution_add_fusion.1 = f32[4,2,8,512]{3,2,1,0:T(8,128)S(1)} fusion(f32[4,2,8,512]{3,2,1,0:T(8,128)S(1)} %fusion.51, f32[4,2,512,512]{3,2,1,0:T(8,128)} %param.10, f32[4,2,8,128]{3,2,1,0:T(8,128)S(1)} %get-tuple-element.37, f32[4,2,8,128]{3,2,1,0:T(8,128)S(1)} %get-tuple-element.36, f32[4,2,8,128]{3,2,1,0:T(8,128)S(1)} %get-tuple-element.38, ...), kind=kOutput, calls=%fused_computation.7 | convolution fusion | flops 201490432 | bytes 8785920 | tf_op jit(solution)/shard_map/abij,ablj->abli/dot_general | solution.py:58
  174.2 1.3 collective-permute-start.6
  176.9 4.7 %collective-permute-start.5 = (f32[1,2,8,512]{3,2,1,0:T(8,128)S(1)}, f32[1,2,8,512]{3,2,1,0:T(8,128)S(1)}, u32[]{:S(2)}, u32[]{:S(2)}) collective-permute-start(f32[1,2,8,512]{3,2,1,0:T(8,128)S(1)} %get-tuple-element.32), channel_id=1, source_target_pairs={{4,0},{8,4},{12,8},{16,12},{20,16},{24,20},{28,24},{0,28},{5,1},{9... | collective-permute-start | bytes 98312 | tf_op jit(solution)/shard_map/ppermute | solution.py:19
  181.6 1.9 collective-permute-done.4
  183.6 9.2 %convolution_subtract_fusion.1 = f32[4,2,8,512]{3,2,1,0:T(8,128)S(1)} fusion(f32[4,2,8,512]{3,2,1,0:T(8,128)S(1)} %copy-done.2, f32[4,2,512,512]{3,2,1,0:T(8,128)} %param.9, f32[4,2,8,128]{3,2,1,0:T(8,128)S(1)} %get-tuple-element.29, f32[4,2,8,128]{3,2,1,0:T(8,128)S(1)} %get-tuple-element.28, f32[4,2,8,128]{3,2,1,0:T(8,128)S(1)} %get-tuple-element.30, ...), kind=kOutput, calls=%fused_computation.6 | convolution fusion | flops 201490432 | bytes 8785920 | tf_op jit(solution)/shard_map/abij,ablj->abli/dot_general | solution.py:58
  192.8 2.5 collective-permute-start.10
  195.3 1.3 collective-permute-start.11
  196.9 4.7 %collective-permute-start.9 = (f32[1,2,8,512]{3,2,1,0:T(8,128)S(1)}, f32[1,2,8,512]{3,2,1,0:T(8,128)S(1)}, u32[]{:S(2)}, u32[]{:S(2)}) collective-permute-start(f32[1,2,8,512]{3,2,1,0:T(8,128)S(1)} %get-tuple-element.24), channel_id=1, source_target_pairs={{4,0},{8,4},{12,8},{16,12},{20,16},{24,20},{28,24},{0,28},{5,1},{9... | collective-permute-start | bytes 98312 | tf_op jit(solution)/shard_map/ppermute | solution.py:19
  201.6 2.0 collective-permute-done.8
  204.1 45.8 %all_gather.18 = f32[8,4096]{1,0:T(8,128)S(1)} all-gather(f32[8,128]{1,0:T(8,128)S(1)} %reshape.38), channel_id=1, replica_groups=mesh['wide'=8,'narrow'=4] {'wide','narrow'}, dimensions={1}, use_global_device_ids=true | all-gather | bytes 135168 | tf_op jit(solution)/shard_map/all_gather | solution.py:86
  250.6 23.5 %scatter_custom_fusion.1 = f32[8,2176]{0,1:T(8,128)} fusion(s32[4096]{0:T(1024)} %compare_select_fusion, f32[4096,8]{1,0:T(8,128)S(1)} %copy.26, f32[]{:T(128)} %constant.4.clone.1), kind=kCustom, calls=%fused_computation.10 | custom fusion | flops 32768 | bytes 70144 | tf_op jit(solution)/shard_map/scatter-add | solution.py:88
  274.1 2.0 fusion.4
  276.1 10.3 %psum.15 = f32[8,272]{1,0:T(8,128)S(1)} all-reduce(f32[8,272]{1,0:T(8,128)S(1)} %fusion.4), channel_id=1, replica_groups=mesh['wide'=8,'narrow'=4] {'narrow'}, use_global_device_ids=true, to_apply=%region_3.5 | all-reduce | flops 2176 | bytes 17408 | tf_op jit(solution)/shard_map/psum | solution.py:96
  286.4 30.5 %all-gather.2 = f32[8,272,8]{1,2,0:T(8,128)S(1)} all-gather(f32[1,272,8]{1,2,0:T(8,128)S(1)} %bitcast.46), channel_id=1, replica_groups=mesh['wide'=8,'narrow'=4] {'wide'}, dimensions={0}, use_global_device_ids=true | all-gather | bytes 78336 | tf_op jit(solution)/shard_map/all_gather | solution.py:97
  318.3 9.2 %convolution_add_fusion = f32[4,2,8,512]{3,2,1,0:T(8,128)S(1)} fusion(f32[4,2,8,512]{3,2,1,0:T(8,128)S(1)} %fusion.52, f32[4,2,512,512]{3,2,1,0:T(8,128)} %param.10, f32[4,2,8,128]{3,2,1,0:T(8,128)S(1)} %get-tuple-element.21, f32[4,2,8,128]{3,2,1,0:T(8,128)S(1)} %get-tuple-element.20, f32[4,2,8,128]{3,2,1,0:T(8,128)S(1)} %copy-done.5, ...), kind=kOutput, calls=%fused_computation.5 | convolution fusion | flops 201490432 | bytes 8785920 | tf_op jit(solution)/shard_map/abij,ablj->abli/dot_general | solution.py:58
  327.6 1.3 collective-permute-start.14
  330.3 4.7 %collective-permute-start.13 = (f32[1,2,8,512]{3,2,1,0:T(8,128)S(1)}, f32[1,2,8,512]{3,2,1,0:T(8,128)S(1)}, u32[]{:S(2)}, u32[]{:S(2)}) collective-permute-start(f32[1,2,8,512]{3,2,1,0:T(8,128)S(1)} %get-tuple-element.16), channel_id=1, source_target_pairs={{4,0},{8,4},{12,8},{16,12},{20,16},{24,20},{28,24},{0,28},{5,1},{9... | collective-permute-start | bytes 98312 | tf_op jit(solution)/shard_map/ppermute | solution.py:19
  335.0 1.9 collective-permute-done.12
  336.9 9.2 %convolution_subtract_fusion = f32[4,2,8,512]{3,2,1,0:T(8,128)S(1)} fusion(f32[4,2,8,512]{3,2,1,0:T(8,128)S(1)} %copy-done.2, f32[4,2,8,512]{3,2,1,0:T(8,128)S(1)} %fusion.8, f32[4,2,512,512]{3,2,1,0:T(8,128)} %param.9), kind=kOutput, calls=%fused_computation.4 | convolution fusion | flops 201359360 | bytes 8781824 | tf_op jit(solution)/shard_map/abij,ablj->abli/dot_general | solution.py:58
  346.2 3.7 %collective-permute-start.18 = (f32[4,1,8,512]{3,2,1,0:T(8,128)S(1)}, f32[4,1,8,512]{3,2,1,0:T(8,128)S(1)}, u32[]{:S(2)}, u32[]{:S(2)}) collective-permute-start(f32[4,1,8,512]{3,2,1,0:T(8,128)S(1)} %get-tuple-element.9), channel_id=1, source_target_pairs={{0,1},{1,2},{2,3},{4,5},{5,6},{6,7},{8,9},{9,10},{10,11},{12,13},{... | collective-permute-start | bytes 196616 | tf_op jit(solution)/shard_map/ppermute | solution.py:16
  351.3 4.7 %collective-permute-start.17 = (f32[1,2,8,512]{3,2,1,0:T(8,128)S(1)}, f32[1,2,8,512]{3,2,1,0:T(8,128)S(1)}, u32[]{:S(2)}, u32[]{:S(2)}) collective-permute-start(f32[1,2,8,512]{3,2,1,0:T(8,128)S(1)} %get-tuple-element.8), channel_id=1, source_target_pairs={{4,0},{8,4},{12,8},{16,12},{20,16},{24,20},{28,24},{0,28},{5,1},{9... | collective-permute-start | bytes 98312 | tf_op jit(solution)/shard_map/ppermute | solution.py:19
  356.0 2.0 collective-permute-done.16
  (84 shorter events, 16.7 us)
Async XLA Ops:
  0.6 118.8 %copy-start = (f32[272,544]{1,0:T(8,128)S(1)}, f32[272,544]{1,0:T(8,128)}, u32[]{:S(2)}) copy-start(f32[272,544]{1,0:T(8,128)} %param.12) | copy-start | bytes 1775620
  1.5 54.5 %collective-permute-start = (f32[1,2,8,512]{3,2,1,0:T(8,128)S(1)}, f32[1,2,8,512]{3,2,1,0:T(8,128)S(1)}, u32[]{:S(2)}, u32[]{:S(2)}) collective-permute-start(f32[1,2,8,512]{3,2,1,0:T(8,128)S(1)} %get-tuple-element.39), channel_id=1, source_target_pairs={{0,4},{4,8},{8,12},{12,16},{16,20},{20,24},{24,28},{28,0},{1,5},{5... | collective-permute-start | bytes 98312 | tf_op jit(solution)/shard_map/ppermute | solution.py:16
  4.5 51.5 %collective-permute-start.1 = (f32[1,2,8,512]{3,2,1,0:T(8,128)S(1)}, f32[1,2,8,512]{3,2,1,0:T(8,128)S(1)}, u32[]{:S(2)}, u32[]{:S(2)}) collective-permute-start(f32[1,2,8,512]{3,2,1,0:T(8,128)S(1)} %get-tuple-element.40), channel_id=1, source_target_pairs={{4,0},{8,4},{12,8},{16,12},{20,16},{24,20},{28,24},{0,28},{5,1},{9... | collective-permute-start | bytes 98312 | tf_op jit(solution)/shard_map/ppermute | solution.py:19
  8.4 47.5 %collective-permute-start.2 = (f32[4,1,8,512]{3,2,1,0:T(8,128)S(1)}, f32[4,1,8,512]{3,2,1,0:T(8,128)S(1)}, u32[]{:S(2)}, u32[]{:S(2)}) collective-permute-start(f32[4,1,8,512]{3,2,1,0:T(8,128)S(1)} %get-tuple-element.41), channel_id=1, source_target_pairs={{0,1},{1,2},{2,3},{4,5},{5,6},{6,7},{8,9},{9,10},{10,11},{12,13},{... | collective-permute-start | bytes 196616 | tf_op jit(solution)/shard_map/ppermute | solution.py:16
  9.9 46.1 %collective-permute-start.3 = (f32[4,1,8,512]{3,2,1,0:T(8,128)S(1)}, f32[4,1,8,512]{3,2,1,0:T(8,128)S(1)}, u32[]{:S(2)}, u32[]{:S(2)}) collective-permute-start(f32[4,1,8,512]{3,2,1,0:T(8,128)S(1)} %get-tuple-element.42), channel_id=1, source_target_pairs={{1,0},{2,1},{3,2},{5,4},{6,5},{7,6},{9,8},{10,9},{11,10},{13,12},{... | collective-permute-start | bytes 196616 | tf_op jit(solution)/shard_map/ppermute | solution.py:19
  95.9 68.6 %copy-start.6 = (pred[128]{0:T(512)(128)(4,1)S(1)}, pred[128]{0:T(512)(128)(4,1)}, u32[]{:S(2)}) copy-start(pred[128]{0:T(512)(128)(4,1)} %compare_and_fusion) | copy-start | bytes 388
  95.9 68.7 %copy-start.1 = (f32[4,2,16,512]{3,2,1,0:T(8,128)S(1)}, f32[4,2,16,512]{3,2,1,0:T(8,128)}, u32[]{:S(2)}) copy-start(f32[4,2,16,512]{3,2,1,0:T(8,128)} %param.11) | copy-start | bytes 786436
  165.0 18.6 %copy-start.2 = (f32[4,2,8,512]{3,2,1,0:T(8,128)S(1)}, f32[4,2,8,512]{3,2,1,0:T(8,128)}, u32[]{:S(2)}) copy-start(f32[4,2,8,512]{3,2,1,0:T(8,128)} %param.8) | copy-start | bytes 393220
  174.2 9.3 %collective-permute-start.6 = (f32[4,1,8,512]{3,2,1,0:T(8,128)S(1)}, f32[4,1,8,512]{3,2,1,0:T(8,128)S(1)}, u32[]{:S(2)}, u32[]{:S(2)}) collective-permute-start(f32[4,1,8,512]{3,2,1,0:T(8,128)S(1)} %get-tuple-element.33), channel_id=1, source_target_pairs={{0,1},{1,2},{2,3},{4,5},{5,6},{6,7},{8,9},{9,10},{10,11},{12,13},{... | collective-permute-start | bytes 196616 | tf_op jit(solution)/shard_map/ppermute | solution.py:16
  175.5 8.0 %collective-permute-start.7 = (f32[4,1,8,512]{3,2,1,0:T(8,128)S(1)}, f32[4,1,8,512]{3,2,1,0:T(8,128)S(1)}, u32[]{:S(2)}, u32[]{:S(2)}) collective-permute-start(f32[4,1,8,512]{3,2,1,0:T(8,128)S(1)} %get-tuple-element.34), channel_id=1, source_target_pairs={{1,0},{2,1},{3,2},{5,4},{6,5},{7,6},{9,8},{10,9},{11,10},{13,12},{... | collective-permute-start | bytes 196616 | tf_op jit(solution)/shard_map/ppermute | solution.py:19
  176.8 6.7 %collective-permute-start.4 = (f32[1,2,8,512]{3,2,1,0:T(8,128)S(1)}, f32[1,2,8,512]{3,2,1,0:T(8,128)S(1)}, u32[]{:S(2)}, u32[]{:S(2)}) collective-permute-start(f32[1,2,8,512]{3,2,1,0:T(8,128)S(1)} %get-tuple-element.31), channel_id=1, source_target_pairs={{0,4},{4,8},{8,12},{12,16},{16,20},{20,24},{24,28},{28,0},{1,5},{5... | collective-permute-start | bytes 98312 | tf_op jit(solution)/shard_map/ppermute | solution.py:16
  176.9 6.6 %collective-permute-start.5 = (f32[1,2,8,512]{3,2,1,0:T(8,128)S(1)}, f32[1,2,8,512]{3,2,1,0:T(8,128)S(1)}, u32[]{:S(2)}, u32[]{:S(2)}) collective-permute-start(f32[1,2,8,512]{3,2,1,0:T(8,128)S(1)} %get-tuple-element.32), channel_id=1, source_target_pairs={{4,0},{8,4},{12,8},{16,12},{20,16},{24,20},{28,24},{0,28},{5,1},{9... | collective-permute-start | bytes 98312 | tf_op jit(solution)/shard_map/ppermute | solution.py:19
  192.8 10.8 %collective-permute-start.10 = (f32[4,1,8,512]{3,2,1,0:T(8,128)S(1)}, f32[4,1,8,512]{3,2,1,0:T(8,128)S(1)}, u32[]{:S(2)}, u32[]{:S(2)}) collective-permute-start(f32[4,1,8,512]{3,2,1,0:T(8,128)S(1)} %get-tuple-element.25), channel_id=1, source_target_pairs={{0,1},{1,2},{2,3},{4,5},{5,6},{6,7},{8,9},{9,10},{10,11},{12,13},{... | collective-permute-start | bytes 196616 | tf_op jit(solution)/shard_map/ppermute | solution.py:16
  195.3 8.3 %collective-permute-start.11 = (f32[4,1,8,512]{3,2,1,0:T(8,128)S(1)}, f32[4,1,8,512]{3,2,1,0:T(8,128)S(1)}, u32[]{:S(2)}, u32[]{:S(2)}) collective-permute-start(f32[4,1,8,512]{3,2,1,0:T(8,128)S(1)} %get-tuple-element.26), channel_id=1, source_target_pairs={{1,0},{2,1},{3,2},{5,4},{6,5},{7,6},{9,8},{10,9},{11,10},{13,12},{... | collective-permute-start | bytes 196616 | tf_op jit(solution)/shard_map/ppermute | solution.py:19
  196.6 7.0 %collective-permute-start.8 = (f32[1,2,8,512]{3,2,1,0:T(8,128)S(1)}, f32[1,2,8,512]{3,2,1,0:T(8,128)S(1)}, u32[]{:S(2)}, u32[]{:S(2)}) collective-permute-start(f32[1,2,8,512]{3,2,1,0:T(8,128)S(1)} %get-tuple-element.23), channel_id=1, source_target_pairs={{0,4},{4,8},{8,12},{12,16},{16,20},{20,24},{24,28},{28,0},{1,5},{5... | collective-permute-start | bytes 98312 | tf_op jit(solution)/shard_map/ppermute | solution.py:16
  196.9 6.7 %collective-permute-start.9 = (f32[1,2,8,512]{3,2,1,0:T(8,128)S(1)}, f32[1,2,8,512]{3,2,1,0:T(8,128)S(1)}, u32[]{:S(2)}, u32[]{:S(2)}) collective-permute-start(f32[1,2,8,512]{3,2,1,0:T(8,128)S(1)} %get-tuple-element.24), channel_id=1, source_target_pairs={{4,0},{8,4},{12,8},{16,12},{20,16},{24,20},{28,24},{0,28},{5,1},{9... | collective-permute-start | bytes 98312 | tf_op jit(solution)/shard_map/ppermute | solution.py:19
  203.6 46.4 %copy-start.4 = (f32[4,2,8,128]{3,2,1,0:T(8,128)}, f32[4,2,8,128]{3,2,1,0:T(8,128)S(1)}, u32[]{:S(2)}) copy-start(f32[4,2,8,128]{3,2,1,0:T(8,128)S(1)} %get-tuple-element.22) | copy-start | bytes 98308
  250.6 67.3 %copy-start.7 = (pred[128]{0:T(512)(128)(4,1)S(1)}, pred[128]{0:T(512)(128)(4,1)}, u32[]{:S(2)}) copy-start(pred[128]{0:T(512)(128)(4,1)} %compare_and_fusion) | copy-start | bytes 388
  250.6 67.7 %copy-start.5 = (f32[4,2,8,128]{3,2,1,0:T(8,128)S(1)}, f32[4,2,8,128]{3,2,1,0:T(8,128)}, u32[]{:S(2)}) copy-start(f32[4,2,8,128]{3,2,1,0:T(8,128)} %copy-done.4) | copy-start | bytes 98308
  327.6 9.3 %collective-permute-start.14 = (f32[4,1,8,512]{3,2,1,0:T(8,128)S(1)}, f32[4,1,8,512]{3,2,1,0:T(8,128)S(1)}, u32[]{:S(2)}, u32[]{:S(2)}) collective-permute-start(f32[4,1,8,512]{3,2,1,0:T(8,128)S(1)} %get-tuple-element.17), channel_id=1, source_target_pairs={{0,1},{1,2},{2,3},{4,5},{5,6},{6,7},{8,9},{9,10},{10,11},{12,13},{... | collective-permute-start | bytes 196616 | tf_op jit(solution)/shard_map/ppermute | solution.py:16
  328.9 8.0 %collective-permute-start.15 = (f32[4,1,8,512]{3,2,1,0:T(8,128)S(1)}, f32[4,1,8,512]{3,2,1,0:T(8,128)S(1)}, u32[]{:S(2)}, u32[]{:S(2)}) collective-permute-start(f32[4,1,8,512]{3,2,1,0:T(8,128)S(1)} %get-tuple-element.18), channel_id=1, source_target_pairs={{1,0},{2,1},{3,2},{5,4},{6,5},{7,6},{9,8},{10,9},{11,10},{13,12},{... | collective-permute-start | bytes 196616 | tf_op jit(solution)/shard_map/ppermute | solution.py:19
  330.2 6.7 %collective-permute-start.12 = (f32[1,2,8,512]{3,2,1,0:T(8,128)S(1)}, f32[1,2,8,512]{3,2,1,0:T(8,128)S(1)}, u32[]{:S(2)}, u32[]{:S(2)}) collective-permute-start(f32[1,2,8,512]{3,2,1,0:T(8,128)S(1)} %get-tuple-element.15), channel_id=1, source_target_pairs={{0,4},{4,8},{8,12},{12,16},{16,20},{20,24},{24,28},{28,0},{1,5},{5... | collective-permute-start | bytes 98312 | tf_op jit(solution)/shard_map/ppermute | solution.py:16
  330.3 6.6 %collective-permute-start.13 = (f32[1,2,8,512]{3,2,1,0:T(8,128)S(1)}, f32[1,2,8,512]{3,2,1,0:T(8,128)S(1)}, u32[]{:S(2)}, u32[]{:S(2)}) collective-permute-start(f32[1,2,8,512]{3,2,1,0:T(8,128)S(1)} %get-tuple-element.16), channel_id=1, source_target_pairs={{4,0},{8,4},{12,8},{16,12},{20,16},{24,20},{28,24},{0,28},{5,1},{9... | collective-permute-start | bytes 98312 | tf_op jit(solution)/shard_map/ppermute | solution.py:19
  336.9 9.2 %copy-start.3 = (f32[4,2,8,512]{3,2,1,0:T(8,128)}, f32[4,2,8,512]{3,2,1,0:T(8,128)S(1)}, u32[]{:S(2)}) copy-start(f32[4,2,8,512]{3,2,1,0:T(8,128)S(1)} %fusion.8) | copy-start | bytes 393220
  346.2 11.8 %collective-permute-start.18 = (f32[4,1,8,512]{3,2,1,0:T(8,128)S(1)}, f32[4,1,8,512]{3,2,1,0:T(8,128)S(1)}, u32[]{:S(2)}, u32[]{:S(2)}) collective-permute-start(f32[4,1,8,512]{3,2,1,0:T(8,128)S(1)} %get-tuple-element.9), channel_id=1, source_target_pairs={{0,1},{1,2},{2,3},{4,5},{5,6},{6,7},{8,9},{9,10},{10,11},{12,13},{... | collective-permute-start | bytes 196616 | tf_op jit(solution)/shard_map/ppermute | solution.py:16
  349.9 8.1 %collective-permute-start.19 = (f32[4,1,8,512]{3,2,1,0:T(8,128)S(1)}, f32[4,1,8,512]{3,2,1,0:T(8,128)S(1)}, u32[]{:S(2)}, u32[]{:S(2)}) collective-permute-start(f32[4,1,8,512]{3,2,1,0:T(8,128)S(1)} %get-tuple-element.10), channel_id=1, source_target_pairs={{1,0},{2,1},{3,2},{5,4},{6,5},{7,6},{9,8},{10,9},{11,10},{13,12},{... | collective-permute-start | bytes 196616 | tf_op jit(solution)/shard_map/ppermute | solution.py:19
  351.2 6.8 %collective-permute-start.16 = (f32[1,2,8,512]{3,2,1,0:T(8,128)S(1)}, f32[1,2,8,512]{3,2,1,0:T(8,128)S(1)}, u32[]{:S(2)}, u32[]{:S(2)}) collective-permute-start(f32[1,2,8,512]{3,2,1,0:T(8,128)S(1)} %get-tuple-element.7), channel_id=1, source_target_pairs={{0,4},{4,8},{8,12},{12,16},{16,20},{20,24},{24,28},{28,0},{1,5},{5... | collective-permute-start | bytes 98312 | tf_op jit(solution)/shard_map/ppermute | solution.py:16
  351.3 6.7 %collective-permute-start.17 = (f32[1,2,8,512]{3,2,1,0:T(8,128)S(1)}, f32[1,2,8,512]{3,2,1,0:T(8,128)S(1)}, u32[]{:S(2)}, u32[]{:S(2)}) collective-permute-start(f32[1,2,8,512]{3,2,1,0:T(8,128)S(1)} %get-tuple-element.8), channel_id=1, source_target_pairs={{4,0},{8,4},{12,8},{16,12},{20,16},{24,20},{28,24},{0,28},{5,1},{9... | collective-permute-start | bytes 98312 | tf_op jit(solution)/shard_map/ppermute | solution.py:19
where the time goes:
time: 362 us; the launch traced here: 359 us
  blocking collectives  208 us (57%)
  other arithmetic  50.1 us (14%)
  matrix products  43.1 us (12%)
  starting transfers between devices  42.1 us (12%)
  waiting for transfers between devices  7.81 us (2%)
  local copies, waits for them, and re-layouts  7.02 us (2%)
    all_gather x2, blocking collectives, per_device(): lax.all_gather(restricted, ('wide', 'narrow'), axis=1, tiled=True)  82.8 us
    all_gather x2, blocking collectives, per_device(): coarse_sol = lax.all_gather(row_block, 'wide', axis=1, tiled=True)  61.1 us
    scatter-add x2, other arithmetic, per_device(): jnp.zeros((load_count, coarse_total), jnp.float32).at[:, all_numbers]  47 us
    all_gather x1, blocking collectives, per_device(): lax.all_gather(local_numbers, ('wide', 'narrow'), axis=0, tiled=True)  41.8 us
    dot_general x4, matrix products, apply_blocks(): jnp.einsum('abij,ablj->abli', blocks, field, precision=lax.Precision.HIGH...  36.9 us
    ppermute x10, starting transfers between devices, padded(): lax.ppermute(lax.slice_in_dim(block, 0, width, axis=dim), axis, backward)  28.4 us
    psum x2, blocking collectives, per_device(): row_block = lax.psum(partial_rows, 'narrow')  21.9 us
    ppermute x10, starting transfers between devices, padded(): lax.ppermute(lax.slice_in_dim(block, block.shape[dim] - width, None, axis...  13.7 us
  transfers between devices with their start and end apart: 20, of which 4 were waited for; matrix products, arithmetic and copies ran while one was open for 1% of the time, Pallas kernels for 0%

commit v1 on v0

v1 whole, which is shorter than its diff:
```python
import functools

import jax
import jax.numpy as jnp
from jax import lax
from jax.experimental import pallas as pl
from jax.experimental.pallas import tpu as pltpu
from jax.sharding import PartitionSpec as P

ITERS = 2
MESH = pl.DeviceIdType.MESH
F32 = jnp.float32
BF16 = jnp.bfloat16
GROUP = 4
LANES = 128


def halves(value):
    high = value.astype(BF16).astype(F32)
    return high, value - high


def stacked(value):
    high, low = halves(value)
    return jnp.concatenate([high, low], axis=0).astype(BF16)


def dot(left, right):
    return jnp.dot(left, right, preferred_element_type=F32)


def dot_t(left, right):
    return lax.dot_general(left, right, (((1,), (1,)), ((), ())), preferred_element_type=F32)


def kernel(
    dims,
    loads_ref,
    schur_ref,
    local_ref,
    basis_ref,
    coarse_ref,
    index_ref,
    solution_ref,
    residual_ref,
    stage,
    local_parts,
    schur_parts,
    coarse_parts,
    picked_rows,
    select,
    basis_parts,
    field,
    weighted_parts,
    smoothed,
    low_faces,
    high_faces,
    south_faces,
    north_faces,
    numbers,
    gathered,
    partials,
    stage_sems,
    face_send,
    face_recv,
    all_send,
    all_recv,
):
    wide_count, narrow_count, sub_circ, sub_across, load_count, dofs, coarse_dofs, rows, columns = dims
    subs = sub_circ * sub_across
    devices = wide_count * narrow_count
    face = dofs // 4
    packed = subs * coarse_dofs
    row_pad = partials.shape[3]
    column_pad = coarse_parts.shape[1]
    wide = lax.axis_index("wide")
    narrow = lax.axis_index("narrow")
    me = wide * narrow_count + narrow
    west = lax.rem(wide + wide_count - 1, wide_count)
    east = lax.rem(wide + 1, wide_count)
    has_south = narrow > 0
    has_north = narrow < narrow_count - 1

    def stage_copy(source, s):
        return pltpu.make_async_copy(source.at[s], stage.at[s], stage_sems.at[s])

    for s in range(subs):
        stage_copy(local_ref, s).start()

    def place(flat):
        return (lax.div(flat, narrow_count), lax.rem(flat, narrow_count))

    barrier = pltpu.get_barrier_semaphore()

    def greet(step, carry):
        pl.semaphore_signal(
            barrier, inc=1, device_id=place(lax.rem(me + step, devices)), device_id_type=MESH
        )
        return carry

    south_faces[...] = jnp.zeros_like(south_faces)
    north_faces[...] = jnp.zeros_like(north_faces)
    numbers[pl.ds(me, 1)] = jnp.broadcast_to(index_ref[...], (1, 8, packed))
    lax.fori_loop(1, devices, greet, 0)

    coarse_parts[...] = jnp.zeros_like(coarse_parts)
    coarse_high, coarse_low = halves(coarse_ref[...])
    coarse_parts[0:rows, 0:columns] = coarse_high.astype(BF16)
    coarse_parts[rows : 2 * rows, 0:columns] = coarse_low.astype(BF16)
    basis_high, basis_low = halves(basis_ref[...])
    basis_parts[0] = basis_high.astype(BF16)
    basis_parts[1] = basis_low.astype(BF16)
    for iteration in range(ITERS):
        partials[iteration, pl.ds(me, 1)] = jnp.zeros((1, load_count, row_pad), F32)

    pl.semaphore_wait(barrier, devices - 1)

    def all_copy(buffer, turn, target):
        return pltpu.make_async_remote_copy(
            src_ref=buffer.at[me],
            dst_ref=buffer.at[me],
            send_sem=all_send.at[turn],
            recv_sem=all_recv.at[turn],
            device_id=target,
            device_id_type=MESH,
        )

    def send_all(buffer, turn):
        def body(step, carry):
            all_copy(buffer, turn, place(lax.rem(me + step, devices))).start()
            return carry

        lax.fori_loop(1, devices, body, 0)

    def others(buffer, turn):
        return pltpu.make_async_remote_copy(
            src_ref=buffer.at[pl.ds(0, devices - 1)],
            dst_ref=buffer.at[pl.ds(0, devices - 1)],
            send_sem=all_send.at[turn],
            recv_sem=all_recv.at[turn],
            device_id=place(lax.rem(me + 1, devices)),
            device_id_type=MESH,
        )

    def face_copies(source, turn):
        def copy(src, dst, send, recv, target):
            return pltpu.make_async_remote_copy(
                src_ref=src,
                dst_ref=dst.at[turn],
                send_sem=face_send.at[turn, send],
                recv_sem=face_recv.at[turn, recv],
                device_id=target,
                device_id_type=MESH,
            )

        to_west = copy(
            source.at[0, :, :, pl.ds(0, face)], high_faces, 0, 1, (west, narrow)
        )
        to_east = copy(
            source.at[sub_circ - 1, :, :, pl.ds(face, face)], low_faces, 1, 0, (east, narrow)
        )
        to_south = copy(
            source.at[:, 0, :, pl.ds(2 * face, face)],
            north_faces,
            2,
            3,
            (wide, jnp.maximum(narrow - 1, 0)),
        )
        to_north = copy(
            source.at[:, sub_across - 1, :, pl.ds(3 * face, face)],
            south_faces,
            3,
            2,
            (wide, jnp.minimum(narrow + 1, narrow_count - 1)),
        )
        return to_west, to_east, to_south, to_north

    def send_faces(source, turn):
        to_west, to_east, to_south, to_north = face_copies(source, turn)
        to_west.start()
        to_east.start()
        pl.when(has_south)(to_south.start)
        pl.when(has_north)(to_north.start)

    def wait_faces(source, turn):
        to_west, to_east, to_south, to_north = face_copies(source, turn)
        to_west.wait_recv()
        to_east.wait_recv()
        pl.when(has_north)(to_south.wait_recv)
        pl.when(has_south)(to_north.wait_recv)

    def drain_faces(source, turn):
        to_west, to_east, to_south, to_north = face_copies(source, turn)
        to_west.wait_send()
        to_east.wait_send()
        pl.when(has_south)(to_south.wait_send)
        pl.when(has_north)(to_north.wait_send)

    def summed(source, turn, a, b):
        own = source[a, b]
        low = source[a - 1, b, :, face : 2 * face] if a > 0 else low_faces[turn, b]
        high = source[a + 1, b, :, 0:face] if a < sub_circ - 1 else high_faces[turn, b]
        south = source[a, b - 1, :, 3 * face :] if b > 0 else south_faces[turn, a]
        north = (
            source[a, b + 1, :, 2 * face : 3 * face]
            if b < sub_across - 1
            else north_faces[turn, a]
        )
        return own + jnp.concatenate([low, high, south, north], axis=1)

    def inv_mult(b):
        south = jnp.where(has_south, 0.5, 1.0) if b == 0 else 0.5
        north = jnp.where(has_north, 0.5, 1.0) if b == sub_across - 1 else 0.5
        lane = lax.broadcasted_iota(jnp.int32, (1, dofs), 1)
        return jnp.where(lane >= 3 * face, north, jnp.where(lane >= 2 * face, south, 0.5))

    def split_stage(target):
        source = local_ref if target is local_parts else schur_ref

        def body(s, carry):
            stage_copy(source, s).wait()
            high, low = halves(stage[s])
            target[0, s] = high.astype(BF16)
            target[1, s] = low.astype(BF16)
            return carry

        lax.fori_loop(0, subs, body, 0)

    def apply_block(parts, s, vector):
        out = dot(vector, parts[0, s]) + dot(vector, parts[1, s])
        return out[0:load_count] + out[load_count:]

    send_faces(loads_ref, 0)
    send_all(numbers, 0)
    split_stage(local_parts)
    for s in range(subs):
        stage_copy(schur_ref, s).start()

    lane_sub = lax.broadcasted_iota(jnp.int32, (subs, load_count, packed), 2)
    own_sub = lax.broadcasted_iota(jnp.int32, (subs, load_count, packed), 0)
    mine = lax.div(lane_sub, coarse_dofs) == own_sub

    def make_operator():
        others(numbers, 0).wait_recv()
        row_ids = lax.broadcasted_iota(jnp.int32, (column_pad, GROUP * packed), 0)

        def body(group, carry):
            numbers_row = jnp.concatenate(
                [numbers[group * GROUP + p, 0:1] for p in range(GROUP)], axis=1
            )
            hot = (row_ids == numbers_row - narrow * columns).astype(F32).astype(BF16)
            picked_rows[group] = dot(coarse_parts[...], hot).astype(BF16)
            return carry

        lax.fori_loop(0, devices // GROUP, body, 0)
        block_ids = lax.broadcasted_iota(jnp.int32, (row_pad, packed), 0)

        def body_select(block, carry):
            local = index_ref[...] - block * rows
            select[block] = (
                ((block_ids == local) & (block_ids < rows)).astype(F32).astype(BF16)
            )
            return carry

        lax.fori_loop(0, wide_count, body_select, 0)

    def source_of(iteration):
        return loads_ref if iteration == 0 else field.at[2 * iteration - 1]

    for iteration in range(ITERS):
        turn = 2 * iteration
        source = source_of(iteration)
        wait_faces(source, turn)
        products = []
        for a in range(sub_circ):
            for b in range(sub_across):
                s = a * sub_across + b
                weighted = summed(source, turn, a, b) * inv_mult(b)
                parts = stacked(weighted)
                weighted_parts[s] = parts
                restricted = dot_t(parts, basis_parts[0]) + dot_t(parts, basis_parts[1])
                products.append(restricted[0:load_count] + restricted[load_count:])
        restricted = jnp.sum(jnp.where(mine, jnp.stack(products), 0.0), axis=0)
        gathered[iteration, pl.ds(me, 1)] = restricted[None]
        send_all(gathered.at[iteration], 1 + 2 * iteration)
        if iteration == 0:
            make_operator()
        for s in range(subs):
            smoothed[s] = apply_block(local_parts, s, weighted_parts[s])
        others(gathered.at[iteration], 1 + 2 * iteration).wait_recv()

        def add_group(group, total):
            vector = jnp.concatenate(
                [gathered[iteration, group * GROUP + p] for p in range(GROUP)], axis=1
            )
            return total + dot_t(stacked(vector), picked_rows[group])

        total = lax.fori_loop(
            0,
            devices // GROUP,
            add_group,
            jnp.zeros((2 * load_count, 2 * rows), F32),
        )
        total = total[0:load_count] + total[load_count:]
        total = total[:, 0:rows] + total[:, rows:]
        partials[iteration, pl.ds(me, 1), :, 0:rows] = total[None]
        send_all(partials.at[iteration], 2 + 2 * iteration)
        if iteration == 0:
            split_stage(schur_parts)
        others(partials.at[iteration], 2 + 2 * iteration).wait_recv()

        def add_block(block, total):
            coarse = partials[iteration, block * narrow_count]
            for n in range(1, narrow_count):
                coarse = coarse + partials[iteration, block * narrow_count + n]
            return total + dot(stacked(coarse), select[block])

        picked = lax.fori_loop(
            0, wide_count, add_block, jnp.zeros((2 * load_count, packed), F32)
        )
        picked = picked[0:load_count] + picked[load_count:]
        spread = jnp.where(mine, picked[None], 0.0).reshape(subs * load_count, packed)
        spread = stacked(spread)
        spread = dot(spread, basis_parts[0]) + dot(spread, basis_parts[1])
        spread = spread[0 : subs * load_count] + spread[subs * load_count :]
        for a in range(sub_circ):
            for b in range(sub_across):
                s = a * sub_across + b
                field[2 * iteration, a, b] = (
                    smoothed[s] + spread[s * load_count : (s + 1) * load_count]
                )
        correction = field.at[2 * iteration]
        send_faces(correction, turn + 1)
        wait_faces(correction, turn + 1)
        for a in range(sub_circ):
            for b in range(sub_across):
                s = a * sub_across + b
                update = summed(correction, turn + 1, a, b) * inv_mult(b)
                if iteration > 0:
                    update = update + solution_ref[a, b]
                solution_ref[a, b] = update
                field[2 * iteration + 1, a, b] = loads_ref[a, b] - apply_block(
                    schur_parts, s, stacked(update)
                )
        send_faces(field.at[2 * iteration + 1], turn + 2)

    last = source_of(ITERS)
    wait_faces(last, 2 * ITERS)
    for a in range(sub_circ):
        for b in range(sub_across):
            residual_ref[a, b] = summed(last, 2 * ITERS, a, b)

    others(numbers, 0).wait_send()
    for iteration in range(ITERS):
        others(gathered.at[iteration], 1 + 2 * iteration).wait_send()
        others(partials.at[iteration], 2 + 2 * iteration).wait_send()
    drain_faces(loads_ref, 0)
    for turn in range(2 * ITERS):
        drain_faces(field.at[turn], turn + 1)


def per_device(wide_count, narrow_count, loads, schur, local_inverse, coarse_basis, coarse_inverse, coarse_index):
    sub_circ, sub_across, load_count, dofs = loads.shape
    coarse_dofs = coarse_basis.shape[2]
    rows, columns = coarse_inverse.shape
    subs = sub_circ * sub_across
    packed = subs * coarse_dofs
    devices = wide_count * narrow_count
    face = dofs // 4
    row_pad = pl.cdiv(rows, LANES) * LANES
    column_pad = pl.cdiv(columns, LANES) * LANES
    turns = 2 * ITERS + 1
    dims = (wide_count, narrow_count, sub_circ, sub_across, load_count, dofs, coarse_dofs, rows, columns)
    vmem = pl.BlockSpec(memory_space=pltpu.VMEM)
    anywhere = pl.BlockSpec(memory_space=pl.ANY)
    shape = jax.ShapeDtypeStruct(loads.shape, F32)
    return tuple(
        pl.pallas_call(
            functools.partial(kernel, dims),
            out_shape=(shape, shape),
            in_specs=[vmem, anywhere, anywhere, vmem, vmem, vmem],
            out_specs=(vmem, vmem),
            scratch_shapes=[
                pltpu.VMEM((subs, dofs, dofs), F32),
                pltpu.VMEM((2, subs, dofs, dofs), BF16),
                pltpu.VMEM((2, subs, dofs, dofs), BF16),
                pltpu.VMEM((2 * rows, column_pad), BF16),
                pltpu.VMEM((devices // GROUP, 2 * rows, GROUP * packed), BF16),
                pltpu.VMEM((wide_count, row_pad, packed), BF16),
                pltpu.VMEM((2, packed, dofs), BF16),
                pltpu.VMEM((2 * ITERS, sub_circ, sub_across, load_count, dofs), F32),
                pltpu.VMEM((subs, 2 * load_count, dofs), BF16),
                pltpu.VMEM((subs, load_count, dofs), F32),
                pltpu.VMEM((turns, sub_across, load_count, face), F32),
                pltpu.VMEM((turns, sub_across, load_count, face), F32),
                pltpu.VMEM((turns, sub_circ, load_count, face), F32),
                pltpu.VMEM((turns, sub_circ, load_count, face), F32),
                pltpu.VMEM((devices, 8, packed), jnp.int32),
                pltpu.VMEM((ITERS, devices, load_count, packed), F32),
                pltpu.VMEM((ITERS, devices, load_count, row_pad), F32),
                pltpu.SemaphoreType.DMA((subs,)),
                pltpu.SemaphoreType.DMA((turns, 4)),
                pltpu.SemaphoreType.DMA((turns, 4)),
                pltpu.SemaphoreType.DMA((turns,)),
                pltpu.SemaphoreType.DMA((turns,)),
            ],
            compiler_params=pltpu.CompilerParams(
                collective_id=0, has_side_effects=True, vmem_limit_bytes=60 * 1024 * 1024
            ),
        )(
            loads,
            schur.reshape(subs, dofs, dofs),
            local_inverse.reshape(subs, dofs, dofs),
            coarse_basis.reshape(packed, dofs),
            coarse_inverse,
            coarse_index.reshape(1, packed),
        )
    )


def solution(mesh):
    return jax.shard_map(
        functools.partial(per_device, mesh.shape["wide"], mesh.shape["narrow"]),
        mesh=mesh,
        in_specs=(
            P("wide", "narrow", None, None),
            P("wide", "narrow", None, None),
            P("wide", "narrow", None, None),
            P("wide", "narrow", None, None),
            P("wide", "narrow"),
            P("wide", "narrow", None),
        ),
        out_specs=(P("wide", "narrow", None, None), P("wide", "narrow", None, None)),
        check_vma=False,
    )
```

time: 362 us -> 76.9 us (0.21)
  blocking collectives: 208 us -> 0 us
  Pallas kernels: 0 us -> 70.9 us
  other arithmetic: 50.1 us -> 0 us
  matrix products: 43.1 us -> 0 us
  starting transfers between devices: 42.1 us -> 0 us
  waiting for transfers between devices: 7.81 us -> 0 us
    all_gather x5 -> x0, blocking collectives: 186 us -> none  [the longest x2 82.8 us: per_device(): lax.all_gather(restricted, ('wide', 'narrow'), axis=1, tiled=True)]
    pallas_call x0 -> x1, Pallas kernels: none -> 70.9 us  [per_device(): pl.pallas_call(functools.partial(kernel, dims), out_shape=(shape, shape),...]
    scatter-add x2 -> x0, other arithmetic: 47 us -> none  [per_device(): jnp.zeros((load_count, coarse_total), jnp.float32).at[:, all_numbers]]
    dot_general x10 -> x0, matrix products: 43.1 us -> none  [the longest x4 36.9 us: apply_blocks(): jnp.einsum('abij,ablj->abli', blocks, field, precision=lax.Precision.HIGH...]
    ppermute x20 -> x0, starting transfers between devices: 42.1 us -> none  [the longest x10 28.4 us: padded(): lax.ppermute(lax.slice_in_dim(block, 0, width, axis=dim), axis, backward)]
    psum x2 -> x0, blocking collectives: 21.9 us -> none  [per_device(): row_block = lax.psum(partial_rows, 'narrow')]
    ppermute x20 -> x0, waiting for transfers between devices: 7.81 us -> none  [the longest x10 7.79 us: padded(): lax.ppermute(lax.slice_in_dim(block, block.shape[dim] - width, None, axis...]
  transfers between devices with their start and end apart: 20 -> 0, of which waited for: 4 -> 0; matrix products, arithmetic and copies ran while one was open for 1% -> 0% of each run, Pallas kernels for 0% -> 0%
where the time goes in v1:
time: 76.9 us; the launch traced here: 75.9 us
  Pallas kernels  70.9 us (92%)
  local copies, waits for them, and re-layouts  4.42 us (6%)
    pallas_call x1, Pallas kernels, per_device(): pl.pallas_call(functools.partial(kernel, dims), out_shape=(shape, shape),...  70.9 us
    unnamed x2, local copies, waits for them, and re-layouts  3.14 us

profile of v1, /device:TPU:0, one launch (start us, length us, event | category | flops | bytes accessed | tf_op | source)
XLA Modules:
  0.0 75.9 jit_solution(17751485338478991278)
XLA Ops:
  0.6 1.3 %reshape.19.index_ref = s32[1,128]{1,0:T(1,128)} reshape(s32[4,2,16]{2,1,0:T(2,128)} %param.11) | data formatting | bytes 1024 | tf_op jit(solution)/shard_map/reshape | solution.py:416
  1.9 70.9 %shard_map.77 = (f32[4,2,8,512]{3,2,1,0:T(8,128)}, f32[4,2,8,512]{3,2,1,0:T(8,128)}) custom-call(f32[4,2,8,512]{3,2,1,0:T(8,128)} %loads_ref.1, f32[8,512,512]{2,1,0:T(8,128)} %bitcast.3, f32[8,512,512]{2,1,0:T(8,128)} %bitcast.4, f32[128,512]{1,0:T(8,128)} %bitcast.5, f32[272,544]{1,0:T(8,128)} %coarse_ref.1, s32[1,128]{1,0:T(1,128)} %reshape.19.index_ref), custom_call_target="tpu_custom_call" | custom-call | tf_op jit(solution)/shard_map/pallas_call | solution.py:378
  72.8 1.6 %copy.10 = f32[4,2,8,512]{3,2,1,0:T(8,128)} copy(f32[4,2,8,512]{3,2,1,0:T(8,128)} %get-tuple-element.4) | data formatting | bytes 262144
  74.4 1.6 %copy.11 = f32[4,2,8,512]{3,2,1,0:T(8,128)} copy(f32[4,2,8,512]{3,2,1,0:T(8,128)} %get-tuple-element.5) | data formatting | bytes 262144

commit v2 on v1

v2 whole, which is shorter than its diff:
```python
import functools

import jax
import jax.numpy as jnp
from jax import lax
from jax.experimental import pallas as pl
from jax.experimental.pallas import tpu as pltpu
from jax.sharding import PartitionSpec as P

ITERS = 2
MESH = pl.DeviceIdType.MESH
F32 = jnp.float32
BF16 = jnp.bfloat16
GROUP = 4
LANES = 128


def halves(value):
    high = value.astype(BF16).astype(F32)
    return high, value - high


def stacked(value):
    high, low = halves(value)
    return jnp.concatenate([high, low], axis=0).astype(BF16)


def dot(left, right):
    return jnp.dot(left, right, preferred_element_type=F32)


def dot_t(left, right):
    return lax.dot_general(left, right, (((1,), (1,)), ((), ())), preferred_element_type=F32)


def kernel(
    dims,
    loads_ref,
    schur_ref,
    local_ref,
    basis_ref,
    coarse_ref,
    index_ref,
    solution_ref,
    residual_ref,
    stage,
    local_parts,
    schur_parts,
    coarse_parts,
    picked_rows,
    select,
    basis_parts,
    halo_parts,
    halo_hoop,
    halo_across,
    field,
    correction,
    weighted_parts,
    smoothed,
    low_faces,
    high_faces,
    south_faces,
    north_faces,
    numbers,
    gathered,
    narrow_rows,
    wide_rows,
    stage_sems,
    face_send,
    face_recv,
    all_send,
    all_recv,
):
    wide_count, narrow_count, sub_circ, sub_across, load_count, dofs, coarse_dofs, rows, columns = dims
    subs = sub_circ * sub_across
    slots = stage.shape[0]
    devices = wide_count * narrow_count
    face = dofs // 4
    packed = subs * coarse_dofs
    row_pad = wide_rows.shape[3]
    column_pad = coarse_parts.shape[1]
    wide = lax.axis_index("wide")
    narrow = lax.axis_index("narrow")

    def wrapped(position, step, count):
        moved = position + step
        return jnp.where(moved >= count, moved - count, moved)

    west = wrapped(wide, wide_count - 1, wide_count)
    east = wrapped(wide, 1, wide_count)
    south = jnp.maximum(narrow - 1, 0)
    north = jnp.minimum(narrow + 1, narrow_count - 1)
    has_south = narrow > 0
    has_north = narrow < narrow_count - 1
    wide_peers = [(wrapped(wide, step, wide_count), narrow) for step in range(1, wide_count)]
    narrow_peers = [(wide, wrapped(narrow, step, narrow_count)) for step in range(1, narrow_count)]

    def stage_copy(source, s):
        q = s if source is local_ref else s + subs
        slot = lax.rem(q, slots)
        return pltpu.make_async_copy(source.at[s], stage.at[slot], stage_sems.at[slot])

    south_faces[...] = jnp.zeros_like(south_faces)
    north_faces[...] = jnp.zeros_like(north_faces)
    halo_hoop[...] = jnp.zeros_like(halo_hoop)
    halo_across[...] = jnp.zeros_like(halo_across)
    barrier = pltpu.get_barrier_semaphore()
    for peer in wide_peers + narrow_peers:
        pl.semaphore_signal(barrier, inc=1, device_id=peer, device_id_type=MESH)
    for s in range(slots):
        stage_copy(local_ref, s).start()

    index_row = jnp.concatenate(
        [index_ref[a, b : b + 1] for a in range(sub_circ) for b in range(sub_across)], axis=1
    )
    numbers[narrow, pl.ds(wide, 1)] = jnp.broadcast_to(index_row, (1, 8, packed))
    coarse_parts[...] = jnp.zeros_like(coarse_parts)
    coarse_high, coarse_low = halves(coarse_ref[...])
    coarse_parts[0:rows, 0:columns] = coarse_high.astype(BF16)
    coarse_parts[rows : 2 * rows, 0:columns] = coarse_low.astype(BF16)
    basis_high, basis_low = halves(basis_ref[...].reshape(packed, dofs))
    basis_parts[0] = basis_high.astype(BF16)
    basis_parts[1] = basis_low.astype(BF16)
    for iteration in range(ITERS):
        narrow_rows[iteration, pl.ds(narrow, 1)] = jnp.zeros((1, load_count, row_pad), F32)

    pl.semaphore_wait(barrier, len(wide_peers) + len(narrow_peers))

    def remote(src, dst, phase, peer):
        return pltpu.make_async_remote_copy(
            src_ref=src,
            dst_ref=dst,
            send_sem=all_send.at[phase],
            recv_sem=all_recv.at[phase],
            device_id=peer,
            device_id_type=MESH,
        )

    def send(block, phase, peers):
        for peer in peers:
            remote(block, block, phase, peer).start()

    def arrivals(slots, phase, peers):
        part = slots.at[pl.ds(0, len(peers))]
        return remote(part, part, phase, peers[0])

    def send_wide(buffer, phase):
        send(buffer.at[narrow, wide], phase, wide_peers)

    def send_narrow(buffer, phase):
        arrivals(buffer.at[narrow], phase, wide_peers).wait_recv()
        send(buffer.at[narrow], phase + 1, narrow_peers)

    def wait_narrow(buffer, phase):
        arrivals(buffer, phase + 1, narrow_peers).wait_recv()

    def face_copies(source, turn):
        def copy(src, dst, send, recv, target):
            return pltpu.make_async_remote_copy(
                src_ref=src,
                dst_ref=dst.at[turn],
                send_sem=face_send.at[turn, send],
                recv_sem=face_recv.at[turn, recv],
                device_id=target,
                device_id_type=MESH,
            )

        to_west = copy(
            source.at[0, :, :, pl.ds(0, face)], high_faces, 0, 1, (west, narrow)
        )
        to_east = copy(
            source.at[sub_circ - 1, :, :, pl.ds(face, face)], low_faces, 1, 0, (east, narrow)
        )
        to_south = copy(
            source.at[:, 0, :, pl.ds(2 * face, face)],
            north_faces,
            2,
            3,
            (wide, south),
        )
        to_north = copy(
            source.at[:, sub_across - 1, :, pl.ds(3 * face, face)],
            south_faces,
            3,
            2,
            (wide, north),
        )
        return to_west, to_east, to_south, to_north

    def halo_copies():
        turn = 2 * ITERS + 1

        def copy(src, dst, send, recv, target):
            return pltpu.make_async_remote_copy(
                src_ref=src,
                dst_ref=dst,
                send_sem=face_send.at[turn, send],
                recv_sem=face_recv.at[turn, recv],
                device_id=target,
                device_id_type=MESH,
            )

        first, last = 0, sub_across - 1
        return (
            copy(basis_ref.at[0, :, :, pl.ds(0, face)], halo_hoop.at[0], 0, 1, (west, narrow)),
            copy(
                basis_ref.at[sub_circ - 1, :, :, pl.ds(face, face)],
                halo_hoop.at[sub_circ - 1],
                1,
                0,
                (east, narrow),
            ),
            copy(
                basis_ref.at[:, first, :, pl.ds(2 * face, face)],
                halo_across.at[:, first],
                2,
                3,
                (wide, south),
            ),
            copy(
                basis_ref.at[:, last, :, pl.ds(3 * face, face)],
                halo_across.at[:, last],
                3,
                2,
                (wide, north),
            ),
        )

    def send_four(copies):
        to_west, to_east, to_south, to_north = copies
        to_west.start()
        to_east.start()
        pl.when(has_south)(to_south.start)
        pl.when(has_north)(to_north.start)

    def wait_four(copies):
        to_west, to_east, to_south, to_north = copies
        to_west.wait_recv()
        to_east.wait_recv()
        pl.when(has_north)(to_south.wait_recv)
        pl.when(has_south)(to_north.wait_recv)

    def drain_four(copies):
        to_west, to_east, to_south, to_north = copies
        to_west.wait_send()
        to_east.wait_send()
        pl.when(has_south)(to_south.wait_send)
        pl.when(has_north)(to_north.wait_send)

    def summed(source, turn, a, b, extra=None):
        def received(faces, which, i, x, y):
            if extra is None:
                return faces[turn, i]
            start = (x * sub_across + y) * load_count
            return faces[turn, i] + extra[which][start : start + load_count]

        own = source[a, b]
        low = (
            source[a - 1, b, :, face : 2 * face]
            if a > 0
            else received(low_faces, 0, b, sub_circ - 1, b)
        )
        high = (
            source[a + 1, b, :, 0:face]
            if a < sub_circ - 1
            else received(high_faces, 0, b, 0, b)
        )
        below = (
            source[a, b - 1, :, 3 * face :]
            if b > 0
            else received(south_faces, 1, a, a, sub_across - 1)
        )
        above = (
            source[a, b + 1, :, 2 * face : 3 * face]
            if b < sub_across - 1
            else received(north_faces, 1, a, a, 0)
        )
        return own + jnp.concatenate([low, high, below, above], axis=1)

    def inv_mult(b):
        below = jnp.where(has_south, 0.5, 1.0) if b == 0 else 0.5
        above = jnp.where(has_north, 0.5, 1.0) if b == sub_across - 1 else 0.5
        lane = lax.broadcasted_iota(jnp.int32, (1, dofs), 1)
        return jnp.where(lane >= 3 * face, above, jnp.where(lane >= 2 * face, below, 0.5))

    def split_stage(target):
        source = local_ref if target is local_parts else schur_ref

        def body(s, carry):
            stage_copy(source, s).wait()
            high, low = halves(stage[lax.rem(s if source is local_ref else s + subs, slots)])
            target[0, s] = high.astype(BF16)
            target[1, s] = low.astype(BF16)
            later = s + slots
            pl.when(later < subs)(lambda: stage_copy(source, later).start())
            if source is local_ref:
                pl.when(later >= subs)(lambda: stage_copy(schur_ref, later - subs).start())
            return carry

        lax.fori_loop(0, subs, body, 0)

    def apply_block(parts, s, vector):
        out = dot(vector, parts[0, s]) + dot(vector, parts[1, s])
        return out[0:load_count] + out[load_count:]

    send_four(face_copies(loads_ref, 0))
    send_wide(numbers, 0)
    send_four(halo_copies())
    split_stage(local_parts)
    send_narrow(numbers, 0)

    lane_sub = lax.broadcasted_iota(jnp.int32, (subs, load_count, packed), 2)
    own_sub = lax.broadcasted_iota(jnp.int32, (subs, load_count, packed), 0)
    mine = (lane_sub >= own_sub * coarse_dofs) & (lane_sub < (own_sub + 1) * coarse_dofs)
    groups = devices // GROUP
    per_row = wide_count // GROUP

    def make_operator():
        wait_narrow(numbers, 0)
        row_ids = lax.broadcasted_iota(jnp.int32, (column_pad, GROUP * packed), 0)

        def body(group, carry):
            n = lax.div(group, per_row)
            w = lax.rem(group, per_row) * GROUP
            numbers_row = jnp.concatenate([numbers[n, w + p, 0:1] for p in range(GROUP)], axis=1)
            hot = (row_ids == numbers_row - narrow * columns).astype(F32).astype(BF16)
            picked_rows[group] = dot(coarse_parts[...], hot).astype(BF16)
            return carry

        lax.fori_loop(0, groups, body, 0)
        block_ids = lax.broadcasted_iota(jnp.int32, (row_pad, 3 * packed), 0)
        lane = lax.broadcasted_iota(jnp.int32, (1, packed), 1)
        hoop = jnp.where(
            lane < sub_across * coarse_dofs, numbers[narrow, east, 0:1], numbers[narrow, west, 0:1]
        )
        lane_across = lax.rem(lane, sub_across * coarse_dofs)
        across = jnp.where(
            lane_across < coarse_dofs, numbers[north, wide, 0:1], numbers[south, wide, 0:1]
        )
        wanted = jnp.concatenate([numbers[narrow, wide, 0:1], hoop, across], axis=1)

        def body_select(block, carry):
            hot = (block_ids == wanted - block * rows) & (block_ids < rows)
            select[block] = hot.astype(F32).astype(BF16)
            return carry

        lax.fori_loop(0, wide_count, body_select, 0)
        wait_four(halo_copies())
        for source, target in ((halo_hoop, 0), (halo_across, 1)):
            high, low = halves(source[...].reshape(packed, face))
            halo_parts[target, 0] = high.astype(BF16)
            halo_parts[target, 1] = low.astype(BF16)

    def spread(values, parts):
        rows_of = stacked(jnp.where(mine, values[None], 0.0).reshape(subs * load_count, packed))
        out = dot(rows_of, parts[0]) + dot(rows_of, parts[1])
        return out[0 : subs * load_count] + out[subs * load_count :]

    def smooth(first, last):
        for s in range(first, last):
            smoothed[iteration, s // sub_across, s % sub_across] = apply_block(
                local_parts, s, weighted_parts[s]
            )

    def unroll_of(count):
        return min(count, 8)

    for iteration in range(ITERS):
        turn = 2 * iteration
        phase = 2 + 4 * iteration
        source = loads_ref if iteration == 0 else field.at[iteration - 1]
        coarse_in = gathered.at[iteration]
        wait_four(face_copies(source, turn))
        for a in range(sub_circ):
            for b in range(sub_across):
                weighted = summed(source, turn, a, b) * inv_mult(b)
                weighted_parts[a * sub_across + b] = stacked(weighted)
        flat = weighted_parts[...].reshape(subs * 2 * load_count, dofs)
        products = dot_t(flat, basis_parts[0]) + dot_t(flat, basis_parts[1])
        products = products.reshape(subs, 2, load_count, packed)
        products = products[:, 0] + products[:, 1]
        restricted = jnp.sum(jnp.where(mine, products, 0.0), axis=0)
        coarse_in[narrow, pl.ds(wide, 1)] = restricted[None]
        send_wide(coarse_in, phase)
        smooth(0, subs // 2)
        send_narrow(coarse_in, phase)
        smooth(subs // 2, subs)
        send_four(face_copies(smoothed.at[iteration], turn + 1))
        if iteration == 0:
            make_operator()
        wait_narrow(coarse_in, phase)

        def add_group(group, total):
            n = lax.div(group, per_row)
            w = lax.rem(group, per_row) * GROUP
            vector = jnp.concatenate([coarse_in[n, w + p] for p in range(GROUP)], axis=1)
            return total + dot_t(stacked(vector), picked_rows[group])

        total = lax.fori_loop(
            0,
            groups,
            add_group,
            jnp.zeros((2 * load_count, 2 * rows), F32),
            unroll=unroll_of(groups),
        )
        total = total[0:load_count] + total[load_count:]
        total = total[:, 0:rows] + total[:, rows:]
        narrow_rows[iteration, pl.ds(narrow, 1), :, 0:rows] = total[None]
        send(narrow_rows.at[iteration, narrow], phase + 2, narrow_peers)
        if iteration == 0:
            split_stage(schur_parts)
        arrivals(narrow_rows.at[iteration], phase + 2, narrow_peers).wait_recv()
        wide_rows[iteration, pl.ds(wide, 1)] = jnp.sum(
            narrow_rows[iteration], axis=0, keepdims=True
        )
        send(wide_rows.at[iteration, wide], phase + 3, wide_peers)
        wait_four(face_copies(smoothed.at[iteration], turn + 1))
        arrivals(wide_rows.at[iteration], phase + 3, wide_peers).wait_recv()

        def add_block(block, total):
            return total + dot(stacked(wide_rows[iteration, block]), select[block])

        picked = lax.fori_loop(
            0,
            wide_count,
            add_block,
            jnp.zeros((2 * load_count, 3 * packed), F32),
            unroll=unroll_of(wide_count),
        )
        picked = picked[0:load_count] + picked[load_count:]
        inner = spread(picked[:, 0:packed], basis_parts)
        extra = (
            spread(picked[:, packed : 2 * packed], halo_parts[0]),
            spread(picked[:, 2 * packed :], halo_parts[1]),
        )
        for a in range(sub_circ):
            for b in range(sub_across):
                start = (a * sub_across + b) * load_count
                correction[a, b] = smoothed[iteration, a, b] + inner[start : start + load_count]
        for a in range(sub_circ):
            for b in range(sub_across):
                update = summed(correction, turn + 1, a, b, extra) * inv_mult(b)
                if iteration > 0:
                    update = update + solution_ref[a, b]
                solution_ref[a, b] = update
                field[iteration, a, b] = loads_ref[a, b] - apply_block(
                    schur_parts, a * sub_across + b, stacked(update)
                )
        send_four(face_copies(field.at[iteration], turn + 2))

    last = field.at[ITERS - 1]
    wait_four(face_copies(last, 2 * ITERS))
    for a in range(sub_circ):
        for b in range(sub_across):
            residual_ref[a, b] = summed(last, 2 * ITERS, a, b)

    arrivals(numbers.at[narrow], 0, wide_peers).wait_send()
    arrivals(numbers, 1, narrow_peers).wait_send()
    for iteration in range(ITERS):
        phase = 2 + 4 * iteration
        arrivals(gathered.at[iteration, narrow], phase, wide_peers).wait_send()
        arrivals(gathered.at[iteration], phase + 1, narrow_peers).wait_send()
        arrivals(narrow_rows.at[iteration], phase + 2, narrow_peers).wait_send()
        arrivals(wide_rows.at[iteration], phase + 3, wide_peers).wait_send()
        drain_four(face_copies(smoothed.at[iteration], 2 * iteration + 1))
        drain_four(face_copies(field.at[iteration], 2 * iteration + 2))
    drain_four(face_copies(loads_ref, 0))
    drain_four(halo_copies())


def per_device(wide_count, narrow_count, loads, schur, local_inverse, coarse_basis, coarse_inverse, coarse_index):
    sub_circ, sub_across, load_count, dofs = loads.shape
    coarse_dofs = coarse_basis.shape[2]
    rows, columns = coarse_inverse.shape
    subs = sub_circ * sub_across
    packed = subs * coarse_dofs
    devices = wide_count * narrow_count
    face = dofs // 4
    row_pad = pl.cdiv(rows, LANES) * LANES
    column_pad = pl.cdiv(columns, LANES) * LANES
    turns = 2 * ITERS + 1
    slots = max(1, subs - 3)
    dims = (wide_count, narrow_count, sub_circ, sub_across, load_count, dofs, coarse_dofs, rows, columns)
    vmem = pl.BlockSpec(memory_space=pltpu.VMEM)
    anywhere = pl.BlockSpec(memory_space=pl.ANY)
    shape = jax.ShapeDtypeStruct(loads.shape, F32)
    return tuple(
        pl.pallas_call(
            functools.partial(kernel, dims),
            out_shape=(shape, shape),
            in_specs=[vmem, anywhere, anywhere, vmem, vmem, vmem],
            out_specs=(vmem, vmem),
            scratch_shapes=[
                pltpu.VMEM((slots, dofs, dofs), F32),
                pltpu.VMEM((2, subs, dofs, dofs), BF16),
                pltpu.VMEM((2, subs, dofs, dofs), BF16),
                pltpu.VMEM((2 * rows, column_pad), BF16),
                pltpu.VMEM((devices // GROUP, 2 * rows, GROUP * packed), BF16),
                pltpu.VMEM((wide_count, row_pad, 3 * packed), BF16),
                pltpu.VMEM((2, packed, dofs), BF16),
                pltpu.VMEM((2, 2, packed, face), BF16),
                pltpu.VMEM((sub_circ, sub_across, coarse_dofs, face), F32),
                pltpu.VMEM((sub_circ, sub_across, coarse_dofs, face), F32),
                pltpu.VMEM((ITERS, *loads.shape), F32),
                pltpu.VMEM(loads.shape, F32),
                pltpu.VMEM((subs, 2 * load_count, dofs), BF16),
                pltpu.VMEM((ITERS, *loads.shape), F32),
                pltpu.VMEM((turns, sub_across, load_count, face), F32),
                pltpu.VMEM((turns, sub_across, load_count, face), F32),
                pltpu.VMEM((turns, sub_circ, load_count, face), F32),
                pltpu.VMEM((turns, sub_circ, load_count, face), F32),
                pltpu.VMEM((narrow_count, wide_count, 8, packed), jnp.int32),
                pltpu.VMEM((ITERS, narrow_count, wide_count, load_count, packed), F32),
                pltpu.VMEM((ITERS, narrow_count, load_count, row_pad), F32),
                pltpu.VMEM((ITERS, wide_count, load_count, row_pad), F32),
                pltpu.SemaphoreType.DMA((slots,)),
                pltpu.SemaphoreType.DMA((turns + 1, 4)),
                pltpu.SemaphoreType.DMA((turns + 1, 4)),
                pltpu.SemaphoreType.DMA((4 * ITERS + 2,)),
                pltpu.SemaphoreType.DMA((4 * ITERS + 2,)),
            ],
            compiler_params=pltpu.CompilerParams(
                collective_id=0, has_side_effects=True, vmem_limit_bytes=60 * 1024 * 1024
            ),
        )(
            loads,
            schur.reshape(subs, dofs, dofs),
            local_inverse.reshape(subs, dofs, dofs),
            coarse_basis,
            coarse_inverse,
            coarse_index,
        )
    )


def solution(mesh):
    return jax.shard_map(
        functools.partial(per_device, mesh.shape["wide"], mesh.shape["narrow"]),
        mesh=mesh,
        in_specs=(
            P("wide", "narrow", None, None),
            P("wide", "narrow", None, None),
            P("wide", "narrow", None, None),
            P("wide", "narrow", None, None),
            P("wide", "narrow"),
            P("wide", "narrow", None),
        ),
        out_specs=(P("wide", "narrow", None, None), P("wide", "narrow", None, None)),
        check_vma=False,
    )
```

time: 76.9 us -> 63.6 us (0.83)
  Pallas kernels: 70.9 us -> 59.6 us
  local copies, waits for them, and re-layouts: 4.42 us -> 3.14 us
    pallas_call x1, Pallas kernels: 70.9 us -> 59.6 us  [per_device(): pl.pallas_call(functools.partial(kernel, dims), out_shape=(shape, shape),...]
    reshape x1 -> x0, local copies, waits for them, and re-layouts: 1.28 us -> none  [per_device(): coarse_index.reshape(1, packed)]
where the time goes in v2:
time: 63.6 us; the launch traced here: 63.4 us
  Pallas kernels  59.6 us (94%)
  local copies, waits for them, and re-layouts  3.14 us (5%)
  between operations  0.64 us (1%)
    pallas_call x1, Pallas kernels, per_device(): pl.pallas_call(functools.partial(kernel, dims), out_shape=(shape, shape),...  59.6 us
    unnamed x2, local copies, waits for them, and re-layouts  3.14 us

profile of v2, /device:TPU:0, one launch (start us, length us, event | category | flops | bytes accessed | tf_op | source)
XLA Modules:
  0.0 63.4 jit_solution(18332455527001433682)
XLA Ops:
  0.6 59.6 %shard_map.77 = (f32[4,2,8,512]{3,2,1,0:T(8,128)}, f32[4,2,8,512]{3,2,1,0:T(8,128)}) custom-call(f32[4,2,8,512]{3,2,1,0:T(8,128)} %loads_ref.1, f32[8,512,512]{2,1,0:T(8,128)} %bitcast.2, f32[8,512,512]{2,1,0:T(8,128)} %bitcast.3, f32[4,2,16,512]{3,2,1,0:T(8,128)} %basis_ref.1, f32[272,544]{1,0:T(8,128)} %coarse_ref.1, s32[4,2,16]{2,1,0:T(2,128)} %index_ref.1), custom_call_target="tpu_custom_call" | custom-call | tf_op jit(solution)/shard_map/pallas_call | solution.py:488
  60.3 1.6 %copy.10 = f32[4,2,8,512]{3,2,1,0:T(8,128)} copy(f32[4,2,8,512]{3,2,1,0:T(8,128)} %get-tuple-element.4) | data formatting | bytes 262144
  61.8 1.6 %copy.11 = f32[4,2,8,512]{3,2,1,0:T(8,128)} copy(f32[4,2,8,512]{3,2,1,0:T(8,128)} %get-tuple-element.5) | data formatting | bytes 262144

commit v3 on v2

--- a/solution.py
+++ b/solution.py
@@ -12,6 +12,7 @@
 F32 = jnp.float32
 BF16 = jnp.bfloat16
 GROUP = 4
+HOT_BYTES = 8 * 1024 * 1024
 LANES = 128
 
 
@@ -47,7 +48,7 @@
     local_parts,
     schur_parts,
     coarse_parts,
-    picked_rows,
+    hot,
     select,
     basis_parts,
     halo_parts,
@@ -62,7 +63,10 @@
     south_faces,
     north_faces,
     numbers,
+    numbers_across,
     gathered,
+    pieces_out,
+    pieces_in,
     narrow_rows,
     wide_rows,
     stage_sems,
@@ -113,7 +117,8 @@
     index_row = jnp.concatenate(
         [index_ref[a, b : b + 1] for a in range(sub_circ) for b in range(sub_across)], axis=1
     )
-    numbers[narrow, pl.ds(wide, 1)] = jnp.broadcast_to(index_row, (1, 8, packed))
+    numbers[pl.ds(wide, 1)] = jnp.broadcast_to(index_row, (1, 8, packed))
+    numbers_across[pl.ds(narrow, 1)] = jnp.broadcast_to(index_row, (1, 8, packed))
     coarse_parts[...] = jnp.zeros_like(coarse_parts)
     coarse_high, coarse_low = halves(coarse_ref[...])
     coarse_parts[0:rows, 0:columns] = coarse_high.astype(BF16)
@@ -143,16 +148,6 @@
     def arrivals(slots, phase, peers):
         part = slots.at[pl.ds(0, len(peers))]
         return remote(part, part, phase, peers[0])
-
-    def send_wide(buffer, phase):
-        send(buffer.at[narrow, wide], phase, wide_peers)
-
-    def send_narrow(buffer, phase):
-        arrivals(buffer.at[narrow], phase, wide_peers).wait_recv()
-        send(buffer.at[narrow], phase + 1, narrow_peers)
-
-    def wait_narrow(buffer, phase):
-        arrivals(buffer, phase + 1, narrow_peers).wait_recv()
 
     def face_copies(source, turn):
         def copy(src, dst, send, recv, target):
@@ -304,40 +299,41 @@
         return out[0:load_count] + out[load_count:]
 
     send_four(face_copies(loads_ref, 0))
-    send_wide(numbers, 0)
+    send(numbers.at[wide], 0, wide_peers)
+    send(numbers_across.at[narrow], 1, narrow_peers)
     send_four(halo_copies())
     split_stage(local_parts)
-    send_narrow(numbers, 0)
 
     lane_sub = lax.broadcasted_iota(jnp.int32, (subs, load_count, packed), 2)
     own_sub = lax.broadcasted_iota(jnp.int32, (subs, load_count, packed), 0)
     mine = (lane_sub >= own_sub * coarse_dofs) & (lane_sub < (own_sub + 1) * coarse_dofs)
-    groups = devices // GROUP
-    per_row = wide_count // GROUP
-
-    def make_operator():
-        wait_narrow(numbers, 0)
-        row_ids = lax.broadcasted_iota(jnp.int32, (column_pad, GROUP * packed), 0)
-
-        def body(group, carry):
-            n = lax.div(group, per_row)
-            w = lax.rem(group, per_row) * GROUP
-            numbers_row = jnp.concatenate([numbers[n, w + p, 0:1] for p in range(GROUP)], axis=1)
-            hot = (row_ids == numbers_row - narrow * columns).astype(F32).astype(BF16)
-            picked_rows[group] = dot(coarse_parts[...], hot).astype(BF16)
-            return carry
-
-        lax.fori_loop(0, groups, body, 0)
+    groups = wide_count // GROUP
+    stored = hot.shape[0] == groups
+    hot_ids = lax.broadcasted_iota(jnp.int32, (column_pad, GROUP * packed), 0)
+
+    def fill(group, slot, n):
+        row = jnp.concatenate([numbers[group * GROUP + p, 0:1] for p in range(GROUP)], axis=1)
+        hot[slot, n] = (hot_ids == row - n * columns).astype(F32).astype(BF16)
+
+    def make_hot():
+        arrivals(numbers, 0, wide_peers).wait_recv()
+        if stored:
+            for group in range(groups):
+                for n in range(narrow_count):
+                    fill(group, group, n)
+
+    def make_select():
+        arrivals(numbers_across, 1, narrow_peers).wait_recv()
         block_ids = lax.broadcasted_iota(jnp.int32, (row_pad, 3 * packed), 0)
         lane = lax.broadcasted_iota(jnp.int32, (1, packed), 1)
         hoop = jnp.where(
-            lane < sub_across * coarse_dofs, numbers[narrow, east, 0:1], numbers[narrow, west, 0:1]
+            lane < sub_across * coarse_dofs, numbers[east, 0:1], numbers[west, 0:1]
         )
         lane_across = lax.rem(lane, sub_across * coarse_dofs)
         across = jnp.where(
-            lane_across < coarse_dofs, numbers[north, wide, 0:1], numbers[south, wide, 0:1]
-        )
-        wanted = jnp.concatenate([numbers[narrow, wide, 0:1], hoop, across], axis=1)
+            lane_across < coarse_dofs, numbers_across[north, 0:1], numbers_across[south, 0:1]
+        )
+        wanted = jnp.concatenate([numbers[wide, 0:1], hoop, across], axis=1)
 
         def body_select(block, carry):
             hot = (block_ids == wanted - block * rows) & (block_ids < rows)
@@ -380,29 +376,46 @@
         products = products.reshape(subs, 2, load_count, packed)
         products = products[:, 0] + products[:, 1]
         restricted = jnp.sum(jnp.where(mine, products, 0.0), axis=0)
-        coarse_in[narrow, pl.ds(wide, 1)] = restricted[None]
-        send_wide(coarse_in, phase)
-        smooth(0, subs // 2)
-        send_narrow(coarse_in, phase)
-        smooth(subs // 2, subs)
-        send_four(face_copies(smoothed.at[iteration], turn + 1))
+        coarse_in[pl.ds(wide, 1)] = restricted[None]
+        send(coarse_in.at[wide], phase, wide_peers)
         if iteration == 0:
-            make_operator()
-        wait_narrow(coarse_in, phase)
-
-        def add_group(group, total):
-            n = lax.div(group, per_row)
-            w = lax.rem(group, per_row) * GROUP
-            vector = jnp.concatenate([coarse_in[n, w + p] for p in range(GROUP)], axis=1)
-            return total + dot_t(stacked(vector), picked_rows[group])
-
-        total = lax.fori_loop(
+            make_hot()
+            smooth(0, subs)
+        else:
+            smooth(0, subs // 2)
+        arrivals(coarse_in, phase, wide_peers).wait_recv()
+
+        def add_group(group, totals):
+            vector = jnp.concatenate([coarse_in[group * GROUP + p] for p in range(GROUP)], axis=1)
+            vector = stacked(vector)
+            sums = []
+            for n in range(narrow_count):
+                if not stored:
+                    fill(group, 0, n)
+                sums.append(totals[n] + dot_t(vector, hot[group if stored else 0, n]))
+            return tuple(sums)
+
+        totals = lax.fori_loop(
             0,
             groups,
             add_group,
-            jnp.zeros((2 * load_count, 2 * rows), F32),
-            unroll=unroll_of(groups),
-        )
+            tuple(jnp.zeros((2 * load_count, column_pad), F32) for _ in range(narrow_count)),
+            unroll=groups if stored else 1,
+        )
+        for n in range(narrow_count):
+            pieces_out[iteration, n] = totals[n][0:load_count] + totals[n][load_count:]
+        for peer in narrow_peers:
+            remote(
+                pieces_out.at[iteration, peer[1]], pieces_in.at[iteration, narrow], phase + 1, peer
+            ).start()
+        pieces_in[iteration, pl.ds(narrow, 1)] = pieces_out[iteration, pl.ds(narrow, 1)]
+        if iteration == 0:
+            make_select()
+        else:
+            smooth(subs // 2, subs)
+        send_four(face_copies(smoothed.at[iteration], turn + 1))
+        arrivals(pieces_in.at[iteration], phase + 1, narrow_peers).wait_recv()
+        total = dot_t(stacked(jnp.sum(pieces_in[iteration], axis=0)), coarse_parts[...])
         total = total[0:load_count] + total[load_count:]
         total = total[:, 0:rows] + total[:, rows:]
         narrow_rows[iteration, pl.ds(narrow, 1), :, 0:rows] = total[None]
@@ -454,18 +467,29 @@
         for b in range(sub_across):
             residual_ref[a, b] = summed(last, 2 * ITERS, a, b)
 
-    arrivals(numbers.at[narrow], 0, wide_peers).wait_send()
-    arrivals(numbers, 1, narrow_peers).wait_send()
+    arrivals(numbers, 0, wide_peers).wait_send()
+    arrivals(numbers_across, 1, narrow_peers).wait_send()
     for iteration in range(ITERS):
         phase = 2 + 4 * iteration
-        arrivals(gathered.at[iteration, narrow], phase, wide_peers).wait_send()
-        arrivals(gathered.at[iteration], phase + 1, narrow_peers).wait_send()
+        arrivals(gathered.at[iteration], phase, wide_peers).wait_send()
+        arrivals(pieces_in.at[iteration], phase + 1, narrow_peers).wait_send()
         arrivals(narrow_rows.at[iteration], phase + 2, narrow_peers).wait_send()
         arrivals(wide_rows.at[iteration], phase + 3, wide_peers).wait_send()
         drain_four(face_copies(smoothed.at[iteration], 2 * iteration + 1))
         drain_four(face_copies(field.at[iteration], 2 * iteration + 2))
     drain_four(face_copies(loads_ref, 0))
     drain_four(halo_copies())
+
+
+def hand_on(solution_in, residual_in, solution_out, residual_out, sems):
+    copies = [
+        pltpu.make_async_copy(solution_in, solution_out, sems.at[0]),
+        pltpu.make_async_copy(residual_in, residual_out, sems.at[1]),
+    ]
+    for copy in copies:
+        copy.start()
+    for copy in copies:
+        copy.wait()
 
 
 def per_device(wide_count, narrow_count, loads, schur, local_inverse, coarse_basis, coarse_inverse, coarse_index):
@@ -479,12 +503,14 @@
     row_pad = pl.cdiv(rows, LANES) * LANES
     column_pad = pl.cdiv(columns, LANES) * LANES
     turns = 2 * ITERS + 1
-    slots = max(1, subs - 3)
+    slots = subs
+    hot_bytes = wide_count * packed * narrow_count * column_pad * 2
+    hot_slots = wide_count // GROUP if hot_bytes <= HOT_BYTES else 1
     dims = (wide_count, narrow_count, sub_circ, sub_across, load_count, dofs, coarse_dofs, rows, columns)
     vmem = pl.BlockSpec(memory_space=pltpu.VMEM)
     anywhere = pl.BlockSpec(memory_space=pl.ANY)
     shape = jax.ShapeDtypeStruct(loads.shape, F32)
-    return tuple(
+    results = (
         pl.pallas_call(
             functools.partial(kernel, dims),
             out_shape=(shape, shape),
@@ -495,7 +521,7 @@
                 pltpu.VMEM((2, subs, dofs, dofs), BF16),
                 pltpu.VMEM((2, subs, dofs, dofs), BF16),
                 pltpu.VMEM((2 * rows, column_pad), BF16),
-                pltpu.VMEM((devices // GROUP, 2 * rows, GROUP * packed), BF16),
+                pltpu.VMEM((hot_slots, narrow_count, column_pad, GROUP * packed), BF16),
                 pltpu.VMEM((wide_count, row_pad, 3 * packed), BF16),
                 pltpu.VMEM((2, packed, dofs), BF16),
                 pltpu.VMEM((2, 2, packed, face), BF16),
@@ -509,8 +535,11 @@
                 pltpu.VMEM((turns, sub_across, load_count, face), F32),
                 pltpu.VMEM((turns, sub_circ, load_count, face), F32),
                 pltpu.VMEM((turns, sub_circ, load_count, face), F32),
-                pltpu.VMEM((narrow_count, wide_count, 8, packed), jnp.int32),
-                pltpu.VMEM((ITERS, narrow_count, wide_count, load_count, packed), F32),
+                pltpu.VMEM((wide_count, 8, packed), jnp.int32),
+                pltpu.VMEM((narrow_count, 8, packed), jnp.int32),
+                pltpu.VMEM((ITERS, wide_count, load_count, packed), F32),
+                pltpu.VMEM((ITERS, narrow_count, load_count, column_pad), F32),
+                pltpu.VMEM((ITERS, narrow_count, load_count, column_pad), F32),
                 pltpu.VMEM((ITERS, narrow_count, load_count, row_pad), F32),
                 pltpu.VMEM((ITERS, wide_count, load_count, row_pad), F32),
                 pltpu.SemaphoreType.DMA((slots,)),
@@ -531,6 +560,16 @@
             coarse_index,
         )
     )
+    return tuple(
+        pl.pallas_call(
+            hand_on,
+            out_shape=(shape, shape),
+            in_specs=[anywhere, anywhere],
+            out_specs=(anywhere, anywhere),
+            scratch_shapes=[pltpu.SemaphoreType.DMA((2,))],
+            compiler_params=pltpu.CompilerParams(vmem_limit_bytes=60 * 1024 * 1024),
+        )(*results)
+    )
 
 
 def solution(mesh):

time: 63.6 us -> 66.3 us (1.042)
  Pallas kernels: 59.6 us -> 65.5 us
  local copies, waits for them, and re-layouts: 3.14 us -> 0 us
    pallas_call x0 -> x1, Pallas kernels: none -> 9.06 us  [per_device(): pl.pallas_call(hand_on, out_shape=(shape, shape), in_specs=[anywhere, any...]
    pallas_call x1, Pallas kernels: 59.6 us -> 56.4 us  [per_device(): pl.pallas_call(functools.partial(kernel, dims), out_shape=(shape, shape),...]
    unnamed x2 -> x0, local copies, waits for them, and re-layouts: 3.14 us -> none
where the time goes in v3:
time: 66.3 us; the launch traced here: 66.1 us
  Pallas kernels  65.5 us (99%)
    pallas_call x1, Pallas kernels, per_device(): pl.pallas_call(functools.partial(kernel, dims), out_shape=(shape, shape),...  56.4 us
    pallas_call x1, Pallas kernels, per_device(): pl.pallas_call(hand_on, out_shape=(shape, shape), in_specs=[anywhere, any...  9.06 us

profile of v3, /device:TPU:0, one launch (start us, length us, event | category | flops | bytes accessed | tf_op | source)
XLA Modules:
  0.0 66.1 jit_solution(10162194460811638785)
XLA Ops:
  0.6 56.4 %shard_map.77 = (f32[4,2,8,512]{3,2,1,0:T(8,128)}, f32[4,2,8,512]{3,2,1,0:T(8,128)}) custom-call(f32[4,2,8,512]{3,2,1,0:T(8,128)} %loads_ref.1, f32[8,512,512]{2,1,0:T(8,128)} %bitcast.2, f32[8,512,512]{2,1,0:T(8,128)} %bitcast.3, f32[4,2,16,512]{3,2,1,0:T(8,128)} %basis_ref.1, f32[272,544]{1,0:T(8,128)} %coarse_ref.1, s32[4,2,16]{2,1,0:T(2,128)} %index_ref.1), custom_call_target="tpu_custom_call" | custom-call | tf_op jit(solution)/shard_map/pallas_call | solution.py:514
  57.0 9.1 %shard_map.78 = (f32[4,2,8,512]{3,2,1,0:T(8,128)}, f32[4,2,8,512]{3,2,1,0:T(8,128)}) custom-call(f32[4,2,8,512]{3,2,1,0:T(8,128)} %get-tuple-element.4.solution_in, f32[4,2,8,512]{3,2,1,0:T(8,128)} %get-tuple-element.5.residual_in), custom_call_target="tpu_custom_call" | custom-call | tf_op jit(solution)/shard_map/pallas_call | solution.py:564

commit v4 on v3

--- a/solution.py
+++ b/solution.py
@@ -126,6 +126,7 @@
     basis_high, basis_low = halves(basis_ref[...].reshape(packed, dofs))
     basis_parts[0] = basis_high.astype(BF16)
     basis_parts[1] = basis_low.astype(BF16)
+    pieces_out[...] = jnp.zeros_like(pieces_out)
     for iteration in range(ITERS):
         narrow_rows[iteration, pl.ds(narrow, 1)] = jnp.zeros((1, load_count, row_pad), F32)
 
@@ -309,22 +310,23 @@
     mine = (lane_sub >= own_sub * coarse_dofs) & (lane_sub < (own_sub + 1) * coarse_dofs)
     groups = wide_count // GROUP
     stored = hot.shape[0] == groups
-    hot_ids = lax.broadcasted_iota(jnp.int32, (column_pad, GROUP * packed), 0)
-
-    def fill(group, slot, n):
+    hot_ids = lax.broadcasted_iota(jnp.int32, (columns, GROUP * packed), 0)
+
+    def fill(group, slot):
         row = jnp.concatenate([numbers[group * GROUP + p, 0:1] for p in range(GROUP)], axis=1)
-        hot[slot, n] = (hot_ids == row - n * columns).astype(F32).astype(BF16)
+        for n in range(narrow_count):
+            block = (hot_ids == row - n * columns).astype(F32).astype(BF16)
+            hot[slot, n * columns : (n + 1) * columns] = block
 
     def make_hot():
         arrivals(numbers, 0, wide_peers).wait_recv()
         if stored:
             for group in range(groups):
-                for n in range(narrow_count):
-                    fill(group, group, n)
+                fill(group, group)
 
     def make_select():
         arrivals(numbers_across, 1, narrow_peers).wait_recv()
-        block_ids = lax.broadcasted_iota(jnp.int32, (row_pad, 3 * packed), 0)
+        block_ids = lax.broadcasted_iota(jnp.int32, (rows, 3 * packed), 0)
         lane = lax.broadcasted_iota(jnp.int32, (1, packed), 1)
         hoop = jnp.where(
             lane < sub_across * coarse_dofs, numbers[east, 0:1], numbers[west, 0:1]
@@ -335,12 +337,9 @@
         )
         wanted = jnp.concatenate([numbers[wide, 0:1], hoop, across], axis=1)
 
-        def body_select(block, carry):
-            hot = (block_ids == wanted - block * rows) & (block_ids < rows)
-            select[block] = hot.astype(F32).astype(BF16)
-            return carry
-
-        lax.fori_loop(0, wide_count, body_select, 0)
+        for block in range(wide_count):
+            chosen = (block_ids == wanted - block * rows).astype(F32).astype(BF16)
+            select[block * rows : (block + 1) * rows] = chosen
         wait_four(halo_copies())
         for source, target in ((halo_hoop, 0), (halo_across, 1)):
             high, low = halves(source[...].reshape(packed, face))
@@ -352,14 +351,13 @@
         out = dot(rows_of, parts[0]) + dot(rows_of, parts[1])
         return out[0 : subs * load_count] + out[subs * load_count :]
 
+    cut = subs // 3
+
     def smooth(first, last):
         for s in range(first, last):
             smoothed[iteration, s // sub_across, s % sub_across] = apply_block(
                 local_parts, s, weighted_parts[s]
             )
-
-    def unroll_of(count):
-        return min(count, 8)
 
     for iteration in range(ITERS):
         turn = 2 * iteration
@@ -380,66 +378,55 @@
         send(coarse_in.at[wide], phase, wide_peers)
         if iteration == 0:
             make_hot()
-            smooth(0, subs)
-        else:
-            smooth(0, subs // 2)
+        smooth(0, cut)
         arrivals(coarse_in, phase, wide_peers).wait_recv()
 
-        def add_group(group, totals):
+        def add_group(group, total):
             vector = jnp.concatenate([coarse_in[group * GROUP + p] for p in range(GROUP)], axis=1)
-            vector = stacked(vector)
-            sums = []
-            for n in range(narrow_count):
-                if not stored:
-                    fill(group, 0, n)
-                sums.append(totals[n] + dot_t(vector, hot[group if stored else 0, n]))
-            return tuple(sums)
-
-        totals = lax.fori_loop(
+            if not stored:
+                fill(group, 0)
+            return total + dot_t(stacked(vector), hot[group if stored else 0])
+
+        total = lax.fori_loop(
             0,
             groups,
             add_group,
-            tuple(jnp.zeros((2 * load_count, column_pad), F32) for _ in range(narrow_count)),
+            jnp.zeros((2 * load_count, narrow_count * columns), F32),
             unroll=groups if stored else 1,
         )
+        total = total[0:load_count] + total[load_count:]
         for n in range(narrow_count):
-            pieces_out[iteration, n] = totals[n][0:load_count] + totals[n][load_count:]
+            pieces_out[iteration, n, :, 0:columns] = total[:, n * columns : (n + 1) * columns]
         for peer in narrow_peers:
             remote(
                 pieces_out.at[iteration, peer[1]], pieces_in.at[iteration, narrow], phase + 1, peer
             ).start()
         pieces_in[iteration, pl.ds(narrow, 1)] = pieces_out[iteration, pl.ds(narrow, 1)]
+        smooth(cut, 2 * cut)
         if iteration == 0:
             make_select()
-        else:
-            smooth(subs // 2, subs)
-        send_four(face_copies(smoothed.at[iteration], turn + 1))
         arrivals(pieces_in.at[iteration], phase + 1, narrow_peers).wait_recv()
         total = dot_t(stacked(jnp.sum(pieces_in[iteration], axis=0)), coarse_parts[...])
         total = total[0:load_count] + total[load_count:]
         total = total[:, 0:rows] + total[:, rows:]
         narrow_rows[iteration, pl.ds(narrow, 1), :, 0:rows] = total[None]
         send(narrow_rows.at[iteration, narrow], phase + 2, narrow_peers)
-        if iteration == 0:
-            split_stage(schur_parts)
+        smooth(2 * cut, subs)
+        send_four(face_copies(smoothed.at[iteration], turn + 1))
         arrivals(narrow_rows.at[iteration], phase + 2, narrow_peers).wait_recv()
         wide_rows[iteration, pl.ds(wide, 1)] = jnp.sum(
             narrow_rows[iteration], axis=0, keepdims=True
         )
         send(wide_rows.at[iteration, wide], phase + 3, wide_peers)
+        if iteration == 0:
+            split_stage(schur_parts)
         wait_four(face_copies(smoothed.at[iteration], turn + 1))
         arrivals(wide_rows.at[iteration], phase + 3, wide_peers).wait_recv()
 
-        def add_block(block, total):
-            return total + dot(stacked(wide_rows[iteration, block]), select[block])
-
-        picked = lax.fori_loop(
-            0,
-            wide_count,
-            add_block,
-            jnp.zeros((2 * load_count, 3 * packed), F32),
-            unroll=unroll_of(wide_count),
-        )
+        coarse = jnp.concatenate(
+            [wide_rows[iteration, block, :, 0:rows] for block in range(wide_count)], axis=1
+        )
+        picked = dot(stacked(coarse), select[...])
         picked = picked[0:load_count] + picked[load_count:]
         inner = spread(picked[:, 0:packed], basis_parts)
         extra = (
@@ -450,7 +437,8 @@
             for b in range(sub_across):
                 start = (a * sub_across + b) * load_count
                 correction[a, b] = smoothed[iteration, a, b] + inner[start : start + load_count]
-        for a in range(sub_circ):
+        to_west, to_east, to_south, to_north = face_copies(field.at[iteration], turn + 2)
+        for a in [0, sub_circ - 1, *range(1, sub_circ - 1)]:
             for b in range(sub_across):
                 update = summed(correction, turn + 1, a, b, extra) * inv_mult(b)
                 if iteration > 0:
@@ -459,7 +447,12 @@
                 field[iteration, a, b] = loads_ref[a, b] - apply_block(
                     schur_parts, a * sub_across + b, stacked(update)
                 )
-        send_four(face_copies(field.at[iteration], turn + 2))
+            if a == 0:
+                to_west.start()
+            if a == sub_circ - 1:
+                to_east.start()
+        pl.when(has_south)(to_south.start)
+        pl.when(has_north)(to_north.start)
 
     last = field.at[ITERS - 1]
     wait_four(face_copies(last, 2 * ITERS))
@@ -481,15 +474,9 @@
     drain_four(halo_copies())
 
 
-def hand_on(solution_in, residual_in, solution_out, residual_out, sems):
-    copies = [
-        pltpu.make_async_copy(solution_in, solution_out, sems.at[0]),
-        pltpu.make_async_copy(residual_in, residual_out, sems.at[1]),
-    ]
-    for copy in copies:
-        copy.start()
-    for copy in copies:
-        copy.wait()
+def hand_on(solution_in, residual_in, solution_out, residual_out):
+    solution_out[...] = solution_in[...]
+    residual_out[...] = residual_in[...]
 
 
 def per_device(wide_count, narrow_count, loads, schur, local_inverse, coarse_basis, coarse_inverse, coarse_index):
@@ -504,7 +491,7 @@
     column_pad = pl.cdiv(columns, LANES) * LANES
     turns = 2 * ITERS + 1
     slots = subs
-    hot_bytes = wide_count * packed * narrow_count * column_pad * 2
+    hot_bytes = wide_count * packed * narrow_count * columns * 2
     hot_slots = wide_count // GROUP if hot_bytes <= HOT_BYTES else 1
     dims = (wide_count, narrow_count, sub_circ, sub_across, load_count, dofs, coarse_dofs, rows, columns)
     vmem = pl.BlockSpec(memory_space=pltpu.VMEM)
@@ -521,8 +508,8 @@
                 pltpu.VMEM((2, subs, dofs, dofs), BF16),
                 pltpu.VMEM((2, subs, dofs, dofs), BF16),
                 pltpu.VMEM((2 * rows, column_pad), BF16),
-                pltpu.VMEM((hot_slots, narrow_count, column_pad, GROUP * packed), BF16),
-                pltpu.VMEM((wide_count, row_pad, 3 * packed), BF16),
+                pltpu.VMEM((hot_slots, narrow_count * columns, GROUP * packed), BF16),
+                pltpu.VMEM((wide_count * rows, 3 * packed), BF16),
                 pltpu.VMEM((2, packed, dofs), BF16),
                 pltpu.VMEM((2, 2, packed, face), BF16),
                 pltpu.VMEM((sub_circ, sub_across, coarse_dofs, face), F32),
@@ -564,9 +551,8 @@
         pl.pallas_call(
             hand_on,
             out_shape=(shape, shape),
-            in_specs=[anywhere, anywhere],
-            out_specs=(anywhere, anywhere),
-            scratch_shapes=[pltpu.SemaphoreType.DMA((2,))],
+            in_specs=[vmem, vmem],
+            out_specs=(vmem, vmem),
             compiler_params=pltpu.CompilerParams(vmem_limit_bytes=60 * 1024 * 1024),
         )(*results)
     )

time: 66.3 us -> 57.9 us (0.87)
  Pallas kernels: 65.5 us -> 56.9 us
    pallas_call x1, Pallas kernels: 9.06 us -> 1.68 us  [per_device(): pl.pallas_call(hand_on, out_shape=(shape, shape), in_specs=[vmem, vmem],...]
    pallas_call x1, Pallas kernels: 56.4 us -> 55.2 us  [per_device(): pl.pallas_call(functools.partial(kernel, dims), out_shape=(shape, shape),...]
where the time goes in v4:
time: 57.9 us; the launch traced here: 57.5 us
  Pallas kernels  56.9 us (98%)
  between operations  0.64 us (1%)
    pallas_call x1, Pallas kernels, per_device(): pl.pallas_call(functools.partial(kernel, dims), out_shape=(shape, shape),...  55.2 us
    pallas_call x1, Pallas kernels, per_device(): pl.pallas_call(hand_on, out_shape=(shape, shape), in_specs=[vmem, vmem],...  1.68 us

profile of v4, /device:TPU:0, one launch (start us, length us, event | category | flops | bytes accessed | tf_op | source)
XLA Modules:
  0.0 57.5 jit_solution(15074027174468290548)
XLA Ops:
  0.6 55.2 %shard_map.77 = (f32[4,2,8,512]{3,2,1,0:T(8,128)}, f32[4,2,8,512]{3,2,1,0:T(8,128)}) custom-call(f32[4,2,8,512]{3,2,1,0:T(8,128)} %loads_ref.1, f32[8,512,512]{2,1,0:T(8,128)} %bitcast.2, f32[8,512,512]{2,1,0:T(8,128)} %bitcast.3, f32[4,2,16,512]{3,2,1,0:T(8,128)} %basis_ref.1, f32[272,544]{1,0:T(8,128)} %coarse_ref.1, s32[4,2,16]{2,1,0:T(2,128)} %index_ref.1), custom_call_target="tpu_custom_call" | custom-call | tf_op jit(solution)/shard_map/pallas_call | solution.py:501
  55.8 1.7 %shard_map.78 = (f32[4,2,8,512]{3,2,1,0:T(8,128)}, f32[4,2,8,512]{3,2,1,0:T(8,128)}) custom-call(f32[4,2,8,512]{3,2,1,0:T(8,128)} %get-tuple-element.4.solution_in, f32[4,2,8,512]{3,2,1,0:T(8,128)} %get-tuple-element.5.residual_in), custom_call_target="tpu_custom_call" | custom-call | tf_op jit(solution)/shard_map/pallas_call | solution.py:551

commit v5 on v4

--- a/solution.py
+++ b/solution.py
@@ -30,20 +30,20 @@
     return jnp.dot(left, right, preferred_element_type=F32)
 
 
-def dot_t(left, right):
-    return lax.dot_general(left, right, (((1,), (1,)), ((), ())), preferred_element_type=F32)
-
-
 def kernel(
     dims,
-    loads_ref,
+    loads_hbm,
     schur_ref,
     local_ref,
-    basis_ref,
-    coarse_ref,
+    basis_hbm,
+    coarse_hbm,
     index_ref,
     solution_ref,
     residual_ref,
+    loads_ref,
+    basis_ref,
+    coarse_ref,
+    coarse_padded,
     stage,
     local_parts,
     schur_parts,
@@ -51,6 +51,7 @@
     hot,
     select,
     basis_parts,
+    basis_turned,
     halo_parts,
     halo_hoop,
     halo_across,
@@ -70,6 +71,7 @@
     narrow_rows,
     wide_rows,
     stage_sems,
+    input_sems,
     face_send,
     face_recv,
     all_send,
@@ -82,7 +84,7 @@
     face = dofs // 4
     packed = subs * coarse_dofs
     row_pad = wide_rows.shape[3]
-    column_pad = coarse_parts.shape[1]
+    column_pad = coarse_parts.shape[0]
     wide = lax.axis_index("wide")
     narrow = lax.axis_index("narrow")
 
@@ -111,6 +113,13 @@
     barrier = pltpu.get_barrier_semaphore()
     for peer in wide_peers + narrow_peers:
         pl.semaphore_signal(barrier, inc=1, device_id=peer, device_id_type=MESH)
+    fetches = (
+        pltpu.make_async_copy(loads_hbm, loads_ref, input_sems.at[0]),
+        pltpu.make_async_copy(basis_hbm, basis_ref, input_sems.at[1]),
+        pltpu.make_async_copy(coarse_hbm, coarse_ref, input_sems.at[2]),
+    )
+    for fetch in fetches:
+        fetch.start()
     for s in range(slots):
         stage_copy(local_ref, s).start()
 
@@ -119,16 +128,7 @@
     )
     numbers[pl.ds(wide, 1)] = jnp.broadcast_to(index_row, (1, 8, packed))
     numbers_across[pl.ds(narrow, 1)] = jnp.broadcast_to(index_row, (1, 8, packed))
-    coarse_parts[...] = jnp.zeros_like(coarse_parts)
-    coarse_high, coarse_low = halves(coarse_ref[...])
-    coarse_parts[0:rows, 0:columns] = coarse_high.astype(BF16)
-    coarse_parts[rows : 2 * rows, 0:columns] = coarse_low.astype(BF16)
-    basis_high, basis_low = halves(basis_ref[...].reshape(packed, dofs))
-    basis_parts[0] = basis_high.astype(BF16)
-    basis_parts[1] = basis_low.astype(BF16)
     pieces_out[...] = jnp.zeros_like(pieces_out)
-    for iteration in range(ITERS):
-        narrow_rows[iteration, pl.ds(narrow, 1)] = jnp.zeros((1, load_count, row_pad), F32)
 
     pl.semaphore_wait(barrier, len(wide_peers) + len(narrow_peers))
 
@@ -198,23 +198,23 @@
 
         first, last = 0, sub_across - 1
         return (
-            copy(basis_ref.at[0, :, :, pl.ds(0, face)], halo_hoop.at[0], 0, 1, (west, narrow)),
+            copy(basis_hbm.at[0, :, :, pl.ds(0, face)], halo_hoop.at[0], 0, 1, (west, narrow)),
             copy(
-                basis_ref.at[sub_circ - 1, :, :, pl.ds(face, face)],
+                basis_hbm.at[sub_circ - 1, :, :, pl.ds(face, face)],
                 halo_hoop.at[sub_circ - 1],
                 1,
                 0,
                 (east, narrow),
             ),
             copy(
-                basis_ref.at[:, first, :, pl.ds(2 * face, face)],
+                basis_hbm.at[:, first, :, pl.ds(2 * face, face)],
                 halo_across.at[:, first],
                 2,
                 3,
                 (wide, south),
             ),
             copy(
-                basis_ref.at[:, last, :, pl.ds(3 * face, face)],
+                basis_hbm.at[:, last, :, pl.ds(3 * face, face)],
                 halo_across.at[:, last],
                 3,
                 2,
@@ -299,24 +299,39 @@
         out = dot(vector, parts[0, s]) + dot(vector, parts[1, s])
         return out[0:load_count] + out[load_count:]
 
-    send_four(face_copies(loads_ref, 0))
+    send_four(face_copies(loads_hbm, 0))
     send(numbers.at[wide], 0, wide_peers)
     send(numbers_across.at[narrow], 1, narrow_peers)
     send_four(halo_copies())
+    fetches[1].wait()
+    basis = basis_ref[...].reshape(packed, dofs)
+    for target, value in ((basis_parts, basis), (basis_turned, basis.T)):
+        high, low = halves(value)
+        target[0] = high.astype(BF16)
+        target[1] = low.astype(BF16)
+    fetches[2].wait()
+    coarse_padded[...] = jnp.zeros_like(coarse_padded)
+    coarse_padded[0:rows, 0:columns] = coarse_ref[...]
+    high, low = halves(coarse_padded[...].T)
+    coarse_parts[:, 0:row_pad] = high.astype(BF16)
+    coarse_parts[:, row_pad:] = low.astype(BF16)
     split_stage(local_parts)
+    fetches[0].wait()
 
     lane_sub = lax.broadcasted_iota(jnp.int32, (subs, load_count, packed), 2)
     own_sub = lax.broadcasted_iota(jnp.int32, (subs, load_count, packed), 0)
     mine = (lane_sub >= own_sub * coarse_dofs) & (lane_sub < (own_sub + 1) * coarse_dofs)
     groups = wide_count // GROUP
     stored = hot.shape[0] == groups
-    hot_ids = lax.broadcasted_iota(jnp.int32, (columns, GROUP * packed), 0)
+    hot_ids = lax.broadcasted_iota(jnp.int32, (packed, LANES), 1)
 
     def fill(group, slot):
-        row = jnp.concatenate([numbers[group * GROUP + p, 0:1] for p in range(GROUP)], axis=1)
-        for n in range(narrow_count):
-            block = (hot_ids == row - n * columns).astype(F32).astype(BF16)
-            hot[slot, n * columns : (n + 1) * columns] = block
+        for p in range(GROUP):
+            row = numbers[group * GROUP + p, 0:1]
+            column = jnp.broadcast_to(row, (LANES, packed)).T
+            for tile in range(hot.shape[2] // LANES):
+                chosen = (column == hot_ids + tile * LANES).astype(F32).astype(BF16)
+                hot[slot, p * packed : (p + 1) * packed, tile * LANES : (tile + 1) * LANES] = chosen
 
     def make_hot():
         arrivals(numbers, 0, wide_peers).wait_recv()
@@ -370,7 +385,7 @@
                 weighted = summed(source, turn, a, b) * inv_mult(b)
                 weighted_parts[a * sub_across + b] = stacked(weighted)
         flat = weighted_parts[...].reshape(subs * 2 * load_count, dofs)
-        products = dot_t(flat, basis_parts[0]) + dot_t(flat, basis_parts[1])
+        products = dot(flat, basis_turned[0]) + dot(flat, basis_turned[1])
         products = products.reshape(subs, 2, load_count, packed)
         products = products[:, 0] + products[:, 1]
         restricted = jnp.sum(jnp.where(mine, products, 0.0), axis=0)
@@ -385,13 +400,13 @@
             vector = jnp.concatenate([coarse_in[group * GROUP + p] for p in range(GROUP)], axis=1)
             if not stored:
                 fill(group, 0)
-            return total + dot_t(stacked(vector), hot[group if stored else 0])
+            return total + dot(stacked(vector), hot[group if stored else 0])
 
         total = lax.fori_loop(
             0,
             groups,
             add_group,
-            jnp.zeros((2 * load_count, narrow_count * columns), F32),
+            jnp.zeros((2 * load_count, hot.shape[2]), F32),
             unroll=groups if stored else 1,
         )
         total = total[0:load_count] + total[load_count:]
@@ -406,10 +421,10 @@
         if iteration == 0:
             make_select()
         arrivals(pieces_in.at[iteration], phase + 1, narrow_peers).wait_recv()
-        total = dot_t(stacked(jnp.sum(pieces_in[iteration], axis=0)), coarse_parts[...])
+        total = dot(stacked(jnp.sum(pieces_in[iteration], axis=0)), coarse_parts[...])
         total = total[0:load_count] + total[load_count:]
-        total = total[:, 0:rows] + total[:, rows:]
-        narrow_rows[iteration, pl.ds(narrow, 1), :, 0:rows] = total[None]
+        total = total[:, 0:row_pad] + total[:, row_pad:]
+        narrow_rows[iteration, pl.ds(narrow, 1)] = total[None]
         send(narrow_rows.at[iteration, narrow], phase + 2, narrow_peers)
         smooth(2 * cut, subs)
         send_four(face_copies(smoothed.at[iteration], turn + 1))
@@ -470,7 +485,7 @@
         arrivals(wide_rows.at[iteration], phase + 3, wide_peers).wait_send()
         drain_four(face_copies(smoothed.at[iteration], 2 * iteration + 1))
         drain_four(face_copies(field.at[iteration], 2 * iteration + 2))
-    drain_four(face_copies(loads_ref, 0))
+    drain_four(face_copies(loads_hbm, 0))
     drain_four(halo_copies())
 
 
@@ -501,16 +516,21 @@
         pl.pallas_call(
             functools.partial(kernel, dims),
             out_shape=(shape, shape),
-            in_specs=[vmem, anywhere, anywhere, vmem, vmem, vmem],
+            in_specs=[anywhere, anywhere, anywhere, anywhere, anywhere, vmem],
             out_specs=(vmem, vmem),
             scratch_shapes=[
+                pltpu.VMEM(loads.shape, F32),
+                pltpu.VMEM(coarse_basis.shape, F32),
+                pltpu.VMEM(coarse_inverse.shape, F32),
+                pltpu.VMEM((row_pad, column_pad), F32),
                 pltpu.VMEM((slots, dofs, dofs), F32),
                 pltpu.VMEM((2, subs, dofs, dofs), BF16),
                 pltpu.VMEM((2, subs, dofs, dofs), BF16),
-                pltpu.VMEM((2 * rows, column_pad), BF16),
-                pltpu.VMEM((hot_slots, narrow_count * columns, GROUP * packed), BF16),
+                pltpu.VMEM((column_pad, 2 * row_pad), BF16),
+                pltpu.VMEM((hot_slots, GROUP * packed, pl.cdiv(narrow_count * columns, LANES) * LANES), BF16),
                 pltpu.VMEM((wide_count * rows, 3 * packed), BF16),
                 pltpu.VMEM((2, packed, dofs), BF16),
+                pltpu.VMEM((2, dofs, packed), BF16),
                 pltpu.VMEM((2, 2, packed, face), BF16),
                 pltpu.VMEM((sub_circ, sub_across, coarse_dofs, face), F32),
                 pltpu.VMEM((sub_circ, sub_across, coarse_dofs, face), F32),
@@ -530,6 +550,7 @@
                 pltpu.VMEM((ITERS, narrow_count, load_count, row_pad), F32),
                 pltpu.VMEM((ITERS, wide_count, load_count, row_pad), F32),
                 pltpu.SemaphoreType.DMA((slots,)),
+                pltpu.SemaphoreType.DMA((3,)),
                 pltpu.SemaphoreType.DMA((turns + 1, 4)),
                 pltpu.SemaphoreType.DMA((turns + 1, 4)),
                 pltpu.SemaphoreType.DMA((4 * ITERS + 2,)),

time: 57.9 us -> 56 us (0.967)
  Pallas kernels: 56.9 us -> 54.9 us
    pallas_call x1, Pallas kernels: 55.2 us -> 53.2 us  [per_device(): pl.pallas_call(functools.partial(kernel, dims), out_shape=(shape, shape),...]
where the time goes in v5:
time: 56 us; the launch traced here: 55.5 us
  Pallas kernels  54.9 us (98%)
  between operations  0.64 us (1%)
    pallas_call x1, Pallas kernels, per_device(): pl.pallas_call(functools.partial(kernel, dims), out_shape=(shape, shape),...  53.2 us
    pallas_call x1, Pallas kernels, per_device(): pl.pallas_call(hand_on, out_shape=(shape, shape), in_specs=[vmem, vmem],...  1.68 us

profile of v5, /device:TPU:0, one launch (start us, length us, event | category | flops | bytes accessed | tf_op | source)
XLA Modules:
  0.0 55.5 jit_solution(12100549128611116665)
XLA Ops:
  0.6 53.2 %shard_map.77 = (f32[4,2,8,512]{3,2,1,0:T(8,128)}, f32[4,2,8,512]{3,2,1,0:T(8,128)}) custom-call(f32[4,2,8,512]{3,2,1,0:T(8,128)} %loads_hbm.1, f32[8,512,512]{2,1,0:T(8,128)} %bitcast.2, f32[8,512,512]{2,1,0:T(8,128)} %bitcast.3, f32[4,2,16,512]{3,2,1,0:T(8,128)} %basis_hbm.1, f32[272,544]{1,0:T(8,128)} %coarse_hbm.1, s32[4,2,16]{2,1,0:T(2,128)} %index_ref.1), custom_call_target="tpu_custom_call" | custom-call | tf_op jit(solution)/shard_map/pallas_call | solution.py:516
  53.8 1.7 %shard_map.78 = (f32[4,2,8,512]{3,2,1,0:T(8,128)}, f32[4,2,8,512]{3,2,1,0:T(8,128)}) custom-call(f32[4,2,8,512]{3,2,1,0:T(8,128)} %get-tuple-element.4.solution_in, f32[4,2,8,512]{3,2,1,0:T(8,128)} %get-tuple-element.5.residual_in), custom_call_target="tpu_custom_call" | custom-call | tf_op jit(solution)/shard_map/pallas_call | solution.py:572

commit v6 on v5

--- a/solution.py
+++ b/solution.py
@@ -315,7 +315,6 @@
     high, low = halves(coarse_padded[...].T)
     coarse_parts[:, 0:row_pad] = high.astype(BF16)
     coarse_parts[:, row_pad:] = low.astype(BF16)
-    split_stage(local_parts)
     fetches[0].wait()
 
     lane_sub = lax.broadcasted_iota(jnp.int32, (subs, load_count, packed), 2)
@@ -392,6 +391,7 @@
         coarse_in[pl.ds(wide, 1)] = restricted[None]
         send(coarse_in.at[wide], phase, wide_peers)
         if iteration == 0:
+            split_stage(local_parts)
             make_hot()
         smooth(0, cut)
         arrivals(coarse_in, phase, wide_peers).wait_recv()

time: 56 us -> 56 us (level)
  no operation moved by 1% of the time
where the time goes in v6:
time: 56 us; the launch traced here: 55.5 us
  Pallas kernels  54.9 us (98%)
  between operations  0.64 us (1%)
    pallas_call x1, Pallas kernels, per_device(): pl.pallas_call(functools.partial(kernel, dims), out_shape=(shape, shape),...  53.2 us
    pallas_call x1, Pallas kernels, per_device(): pl.pallas_call(hand_on, out_shape=(shape, shape), in_specs=[vmem, vmem],...  1.68 us

profile of v6, /device:TPU:0, one launch (start us, length us, event | category | flops | bytes accessed | tf_op | source)
XLA Modules:
  0.0 55.5 jit_solution(13766092675154687017)
XLA Ops:
  0.6 53.2 %shard_map.77 = (f32[4,2,8,512]{3,2,1,0:T(8,128)}, f32[4,2,8,512]{3,2,1,0:T(8,128)}) custom-call(f32[4,2,8,512]{3,2,1,0:T(8,128)} %loads_hbm.1, f32[8,512,512]{2,1,0:T(8,128)} %bitcast.2, f32[8,512,512]{2,1,0:T(8,128)} %bitcast.3, f32[4,2,16,512]{3,2,1,0:T(8,128)} %basis_hbm.1, f32[272,544]{1,0:T(8,128)} %coarse_hbm.1, s32[4,2,16]{2,1,0:T(2,128)} %index_ref.1), custom_call_target="tpu_custom_call" | custom-call | tf_op jit(solution)/shard_map/pallas_call | solution.py:516
  53.8 1.7 %shard_map.78 = (f32[4,2,8,512]{3,2,1,0:T(8,128)}, f32[4,2,8,512]{3,2,1,0:T(8,128)}) custom-call(f32[4,2,8,512]{3,2,1,0:T(8,128)} %get-tuple-element.4.solution_in, f32[4,2,8,512]{3,2,1,0:T(8,128)} %get-tuple-element.5.residual_in), custom_call_target="tpu_custom_call" | custom-call | tf_op jit(solution)/shard_map/pallas_call | solution.py:572
